TPU v7x, 32 devices: a whole 2x2x4 slice. The times are simulated.
32 devices in a mesh: groups: 2 (over x), pool: 2 (over core), tensor: 8 (over z, y).
Axes of the slice: x: 2, y: 2, z: 4, core: 2. Of those that a mesh axis runs over, the one named last changes fastest.
Arguments:
- hidden: bfloat16 [768, 8192], P('groups', ('pool', 'tensor')), parts along dimension 0, may hold values from -6 to 6
- norm_gain: float32 [8192], replicated, may hold values from 0.1 to 1.9
- w_query: bfloat16 [8192, 8192], P(None, ('pool', 'tensor')), may hold values from -0.0625 to 0.0625
- w_out: bfloat16 [8192, 8192], P(('pool', 'tensor')), may hold values from -1.5 to 1.5
- kv_pool: bfloat16 [64, 8, 2, 128, 128], P(('groups', 'pool', 'tensor')), parts along dimension 0
- draft_kv: bfloat16 [768, 2, 1024], P('groups'), parts along dimension 0, may hold values from -10 to 10
- block_table: int32 [8, 8], P('groups'), parts along dimension 0, may hold values from 0 to 31, as said below
- cached_len: int32 [8], P('groups'), parts along dimension 0, may hold values from 897 to 1024, as said below
- draft_pos: int32 [8, 96], P('groups'), parts along dimension 0, may hold values from 0 to 95, as said below
Outputs:
- attended: bfloat16 [768, 8192], P('groups'), parts along dimension 0
There are 2 independent parts, one for each index of `groups`. A program takes and returns all parts, laid end to end along the dimension named above; an argument that names none is the same for every part. Nothing has to cross between parts.
Inputs may be any that keep to these rules, and one draw needn't show every extreme that they name: `block_table`: every pool block appears exactly once in the table. `cached_len`: each request's cached tokens end inside its last listed block; some request holds 1024 cached tokens. `draft_pos`: 0 for a request's first draft token, then rising by 0 or 1 from token to token; in some request it rises by 1 at every token.
All inputs are finite; a program needn't handle non-finite values.
Results may differ from a plain program's by a relative error of at most 0.006.
The roundings to bfloat16 on the way count: a program that leaves them out, or rounds other values in their place, can miss the bound.
Values may be sent and summed in bfloat16 or wider, within the bound.
A program may use at most 128 MiB of HBM per device.

v0:
```python
import jax
import jax.numpy as jnp
from jax import lax
from jax.sharding import PartitionSpec as P


def rotate(values, positions):
    half_dim = values.shape[-1] // 2
    frequency = 500000.0 ** (-(jnp.arange(half_dim, dtype=jnp.float32) * 2.0) / values.shape[-1])
    angles = positions.astype(jnp.float32)[:, None] * frequency[None, :]
    cosine = jnp.cos(angles)[:, None, :]
    sine_part = jnp.sin(angles)[:, None, :]
    first_half = values[..., :half_dim]
    second_half = values[..., half_dim:]
    return jnp.concatenate(
        [
            first_half * cosine - second_half * sine_part,
            second_half * cosine + first_half * sine_part,
        ],
        axis=-1,
    )


def shards(
    hidden, norm_gain, w_query, w_out, kv_pool, draft_kv, block_table, cached_len, draft_pos
):
    devices = lax.axis_size(("pool", "tensor"))
    my_rank = lax.axis_index(("pool", "tensor"))
    block_count = kv_pool.shape[0]
    kv_heads = kv_pool.shape[1]
    block_len = kv_pool.shape[3]
    head_dim = kv_pool.shape[4]
    requests = draft_pos.shape[0]
    drafts = draft_pos.shape[1]
    listed = block_table.shape[1]
    context = listed * block_len
    local_heads = w_query.shape[1] // head_dim
    group_size = devices // kv_heads
    own_head = my_rank // group_size
    whole = lax.all_gather(hidden, ("pool", "tensor"), axis=1, tiled=True).astype(jnp.float32)
    normed_rows = (
        whole * lax.rsqrt(jnp.mean(whole * whole, axis=-1, keepdims=True) + 1e-05) * norm_gain
    ).astype(jnp.bfloat16)
    raw_queries = jnp.dot(normed_rows, w_query, preferred_element_type=jnp.float32)
    positions = (cached_len[:, None] + draft_pos).reshape(-1)
    query_heads = (
        rotate(raw_queries.reshape(-1, local_heads, head_dim), positions) * head_dim ** (-0.5)
    ).astype(jnp.bfloat16)
    query_heads = query_heads.reshape(requests, drafts, local_heads, head_dim)
    owner_rank = block_table // block_count
    local_slot = block_table % block_count
    own_draft = lax.dynamic_slice_in_dim(draft_kv, own_head * head_dim, head_dim, axis=2)
    own_draft = own_draft.reshape(requests, drafts, 2, head_dim)
    draft_keys = own_draft[:, :, 0]
    draft_values = own_draft[:, :, 1]
    draft_valid = (draft_pos[:, None, :] < draft_pos[:, :, None]) | jnp.eye(drafts, dtype=bool)[
        None
    ]
    send_blocks = jnp.broadcast_to(
        kv_pool[:, :, None], (block_count, kv_heads, group_size, 2, block_len, head_dim)
    )
    send_blocks = send_blocks.reshape(block_count, devices, 2, block_len, head_dim)
    arrived = lax.all_to_all(
        send_blocks, ("pool", "tensor"), split_axis=1, concat_axis=1, tiled=True
    )
    slot_index = local_slot * devices + owner_rank
    arrived = arrived.reshape(-1, 2, block_len, head_dim)
    gathered_blocks = arrived[slot_index]
    cache_keys = gathered_blocks[:, :, 0].reshape(requests, context, head_dim)
    cache_values = gathered_blocks[:, :, 1].reshape(requests, context, head_dim)
    cache_scores = jnp.einsum(
        "rqhd,rkd->rqhk", query_heads, cache_keys, preferred_element_type=jnp.float32
    )
    cache_valid = jnp.arange(context)[None, :] < cached_len[:, None]
    cache_scores = jnp.where(cache_valid[:, None, None, :], cache_scores, -jnp.inf)
    draft_scores = jnp.einsum(
        "rqhd,rpd->rqhp", query_heads, draft_keys, preferred_element_type=jnp.float32
    )
    draft_scores = jnp.where(draft_valid[:, :, None, :], draft_scores, -jnp.inf)
    row_peak = jnp.maximum(
        jnp.max(cache_scores, axis=-1, keepdims=True), jnp.max(draft_scores, axis=-1, keepdims=True)
    )
    cache_weights = jnp.exp(cache_scores - row_peak)
    draft_weights = jnp.exp(draft_scores - row_peak)
    weight_sum = jnp.sum(cache_weights, axis=-1, keepdims=True) + jnp.sum(
        draft_weights, axis=-1, keepdims=True
    )
    cache_probs = (cache_weights / weight_sum).astype(jnp.bfloat16)
    draft_probs = (draft_weights / weight_sum).astype(jnp.bfloat16)
    head_rows = jnp.einsum(
        "rqhk,rkd->rqhd", cache_probs, cache_values, preferred_element_type=jnp.float32
    )
    head_rows = head_rows + jnp.einsum(
        "rqhp,rpd->rqhd", draft_probs, draft_values, preferred_element_type=jnp.float32
    )
    heads_out = head_rows.astype(jnp.bfloat16).reshape(requests * drafts, local_heads * head_dim)
    partial_out = jnp.dot(heads_out, w_out, preferred_element_type=jnp.float32)
    result = lax.psum(partial_out, ("pool", "tensor")).astype(jnp.bfloat16)
    return result


def solution(mesh):
    placed = (
        P("groups", ("pool", "tensor")),
        P(),
        P(None, ("pool", "tensor")),
        P(("pool", "tensor"), None),
        P(("groups", "pool", "tensor"), None, None, None, None),
        P("groups", None, None),
        P("groups", None),
        P("groups"),
        P("groups", None),
    )
    return jax.shard_map(
        shards, mesh=mesh, in_specs=placed, out_specs=P("groups", None), check_vma=False
    )
```

profile of v0, /device:TPU:0, one launch (start us, length us, event | category | flops | bytes accessed | tf_op | source)
XLA Modules:
  0.0 663.9 jit_solution(5900251571173676753)
XLA Ops:
  6.6 0.7 all-gather.2.cloned.1.call-update
  7.3 1.3 copy.25
  8.6 1.8 broadcast_in_dim.21
  10.4 7.4 %all-to-all-start = ((bf16[2,16,2,128,128]{4,3,2,0,1:T(8,128)(2,1)}), bf16[2,16,2,128,128]{4,3,2,0,1:T(8,128)(2,1)}, u32[]{:S(2)}, u32[]{:S(2)}) async-start(bf16[2,16,2,128,128]{4,3,2,0,1:T(8,128)(2,1)} %bitcast.50), calls=%async_computation | async-start | bytes 4194304 | tf_op jit(solution)/shard_map/all_to_all | solution.py:63
  18.6 0.4 multiply_cosine_fusion
  19.0 80.3 %all-to-all-done = bf16[2,16,2,128,128]{4,3,2,0,1:T(8,128)(2,1)} async-done(((bf16[2,16,2,128,128]{4,3,2,0,1:T(8,128)(2,1)}), bf16[2,16,2,128,128]{4,3,2,0,1:T(8,128)(2,1)}, u32[]{:S(2)}, u32[]{:S(2)}) %all-to-all-start) | async-done | bytes 2097184 | tf_op jit(solution)/shard_map/all_to_all | solution.py:63
  99.3 3.2 copy.26
  102.4 3.7 gather_fusion
  106.2 2.8 fusion.22
  109.0 4.3 fusion
  113.2 0.3 copy-done.2
  113.6 7.6 %fusion.3 = f32[384,512]{0,1:T(8,128)S(1)} fusion(bf16[8192,512]{1,0:T(8,128)(2,1)} %param.11, bf16[384,8192]{1,0:T(8,128)(2,1)S(1)} %copy-done.2, f32[8192]{0:T(1024)S(1)} %copy-done.7, f32[384]{0:T(512)S(1)} %add_rsqrt_fusion), kind=kOutput, calls=%fused_computation.6 | convolution fusion | flops 3233808384 | bytes 15500800 | tf_op jit(solution)/shard_map/reshape | solution.py:47
  121.3 0.3 concatenate.8
  121.6 0.3 copy.23
  121.9 0.3 concatenate.9
  122.3 0.3 copy.24
  122.6 0.3 fusion.10
  122.8 0.4 fusion.23
  123.3 1.1 select_reduce_fusion
  124.5 1.3 fusion.7
  125.9 2.0 fusion.8
  127.9 0.3 fusion.9
  128.5 6.4 fusion.12
  134.9 522.2 %all-reduce.1 = bf16[384,8192]{1,0:T(8,128)(2,1)} all-reduce(f32[384,8192]{1,0:T(8,128)} %fusion.12), channel_id=1, replica_groups=mesh['groups'=2,'pool'=2,'tensor'=8] {'pool','tensor'}, use_global_device_ids=true, to_apply=%region_5.6 | all-reduce | flops 3145728 | bytes 18874368 | tf_op jit(solution)/shard_map/psum | solution.py:98
  (39 shorter events, 1.2 us)
Async XLA Ops:
  6.5 11.6 %copy-start = (bf16[384,2,1024]{2,1,0:T(2,128)(2,1)S(1)}, bf16[384,2,1024]{2,1,0:T(2,128)(2,1)}, u32[]{:S(2)}) copy-start(bf16[384,2,1024]{2,1,0:T(2,128)(2,1)} %param.14) | copy-start | bytes 4718596
  6.5 11.3 %copy-start.6 = (s32[4,8]{1,0:T(4,128)S(1)}, s32[4,8]{1,0:T(4,128)}, u32[]{:S(2)}) copy-start(s32[4,8]{1,0:T(4,128)} %param.15) | copy-start | bytes 388
  6.5 11.4 %copy-start.4 = (s32[4,96]{1,0:T(4,128)S(1)}, s32[4,96]{1,0:T(4,128)}, u32[]{:S(2)}) copy-start(s32[4,96]{1,0:T(4,128)} %param.17) | copy-start | bytes 4612
  6.5 11.4 %copy-start.5 = (s32[4]{0:T(128)S(1)}, s32[4]{0:T(128)}, u32[]{:S(2)}) copy-start(s32[4]{0:T(128)} %param.16) | copy-start | bytes 52
  6.5 102.4 %all-gather.2.cloned.1.call-start = ((), (), s32[]{:S(2)}) async-start(), calls=%async_computation.1 | async-start | bytes 6684672 | tf_op jit(solution)/shard_map/all_gather | solution.py:40
  10.4 88.9 %all-to-all-start = ((bf16[2,16,2,128,128]{4,3,2,0,1:T(8,128)(2,1)}), bf16[2,16,2,128,128]{4,3,2,0,1:T(8,128)(2,1)}, u32[]{:S(2)}, u32[]{:S(2)}) async-start(bf16[2,16,2,128,128]{4,3,2,0,1:T(8,128)(2,1)} %bitcast.50), calls=%async_computation | async-start | bytes 4194304 | tf_op jit(solution)/shard_map/all_to_all | solution.py:63
  106.2 7.0 %copy-start.7 = (f32[8192]{0:T(1024)S(1)}, f32[8192]{0:T(1024)}, u32[]{:S(2)}) copy-start(f32[8192]{0:T(1024)} %param.10) | copy-start | bytes 98308
  109.0 4.6 copy-start.2
  124.3 1.6 copy-start.3
  124.5 3.9 slice-start
  125.9 2.6 slice-start.1
  128.5 528.6 %copy-start.1 = (bf16[384,2,1024]{2,1,0:T(2,128)(2,1)S(1)}, bf16[384,2,1024]{2,1,0:T(2,128)(2,1)}, u32[]{:S(2)}) copy-start(bf16[384,2,1024]{2,1,0:T(2,128)(2,1)} %param.14) | copy-start | bytes 4718596
Sparse Core Ops, SparseCore 0:
  9.5 98.0 all-gather.1
where the time goes:
time: 664 us
  blocking collectives  522 us (79%)
  waiting for transfers between devices  81 us (12%)
  matrix products  17.8 us (3%)
  local copies, waits for them, and re-layouts  14.9 us (2%)
  between operations  13.7 us (2%)
  starting transfers between devices  7.47 us (1%)
  other arithmetic  6.89 us (1%)
    psum x1, blocking collectives, shards(): result = lax.psum(partial_out, ('pool', 'tensor')).astype(jnp.bfloat16)  522 us
    all_to_all x1, waiting for transfers between devices, shards(): lax.all_to_all(send_blocks, ('pool', 'tensor'), split_axis=1, concat_axis...  80.3 us
  transfers between devices with their start and end apart: 2, of which 1 were waited for; matrix products, arithmetic and copies ran while one was open for 2% of the time, Pallas kernels for 0%

commit v1 on v0

--- a/solution.py
+++ b/solution.py
@@ -1,7 +1,13 @@
+import functools
+
 import jax
 import jax.numpy as jnp
 from jax import lax
+from jax.experimental import pallas as pl
+from jax.experimental.pallas import tpu as pltpu
 from jax.sharding import PartitionSpec as P
+
+VMEM_LIMIT = 56 * 1024 * 1024
 
 
 def rotate(values, positions):
@@ -21,12 +27,377 @@
     )
 
 
+class Place:
+    def __init__(self, ny, nt):
+        self.ny, self.nz, self.nt = ny, nt // ny, nt
+        self.p = lax.axis_index("pool")
+        self.t = lax.axis_index("tensor")
+        self.y = lax.rem(self.t, ny)
+        self.z = self.t // ny
+
+    def chip(self, z, y):
+        return z * self.ny + y
+
+    def up(self, z, by):
+        return lax.rem(z + by, self.nz)
+
+    def down(self, z, by):
+        return lax.rem(z + self.nz - by, self.nz)
+
+    def rank(self, p, t):
+        return p * self.nt + t
+
+    @property
+    def mate(self):
+        return {"pool": 1 - self.p, "tensor": self.t}
+
+    @property
+    def across(self):
+        return {"pool": self.p, "tensor": self.chip(self.z, 1 - self.y)}
+
+    @property
+    def next(self):
+        return {"pool": self.p, "tensor": self.chip(self.up(self.z, 1), self.y)}
+
+    @property
+    def previous(self):
+        return {"pool": self.p, "tensor": self.chip(self.down(self.z, 1), self.y)}
+
+
+def remote(src, dst, send, recv, device):
+    return pltpu.make_async_remote_copy(
+        src_ref=src,
+        dst_ref=dst,
+        send_sem=send,
+        recv_sem=recv,
+        device_id=device,
+        device_id_type=pl.DeviceIdType.MESH,
+    )
+
+
+def meet(devices):
+    barrier = pltpu.get_barrier_semaphore()
+    for device in devices:
+        pl.semaphore_signal(barrier, inc=1, device_id=device, device_id_type=pl.DeviceIdType.MESH)
+    pl.semaphore_wait(barrier, len(devices))
+
+
+def gather_columns(at, own, out, width, sems):
+    zs, zr, ys, yr, ms, mr, ls = sems
+    nz, ny = at.nz, at.ny
+
+    def block(p, z, y):
+        start = pl.multiple_of(at.rank(p, at.chip(z, y)) * width, width)
+        return out.at[:, pl.ds(start, width)]
+
+    keep = pltpu.make_async_copy(own, block(at.p, at.z, at.y), ls)
+    keep.start()
+    started = []
+
+    def ring(s):
+        z = at.down(at.z, s)
+        here = block(at.p, z, at.y)
+        src = own if s == 0 else here
+        if s > 0:
+            remote(here, here, zs.at[s - 1], zr.at[s - 1], at.previous).wait_recv()
+        if s < nz - 1:
+            started.append(remote(src, here, zs.at[s], zr.at[s], at.next))
+            started[-1].start()
+        if ny == 2:
+            started.append(remote(src, here, ys.at[s], yr.at[s], at.across))
+            started[-1].start()
+        started.append(remote(src, here, ms.at[s], mr.at[s], at.mate))
+        started[-1].start()
+
+    def from_across(s):
+        if ny == 2:
+            there = block(at.p, at.down(at.z, s), 1 - at.y)
+            remote(there, there, ys.at[s], yr.at[s], at.across).wait_recv()
+            started.append(remote(there, there, ms.at[nz + s], mr.at[nz + s], at.mate))
+            started[-1].start()
+
+    def finish():
+        for s in range(nz):
+            z = at.down(at.z, s)
+            for y_at in range(ny):
+                y = at.y if y_at == 0 else 1 - at.y
+                there = block(1 - at.p, z, y)
+                slot = s + y_at * nz
+                remote(there, there, ms.at[slot], mr.at[slot], at.mate).wait_recv()
+        for copy in started:
+            copy.wait_send()
+        keep.wait()
+
+    return ring, from_across, finish
+
+
+def gather_sems(ny, nz):
+    dma = pltpu.SemaphoreType.DMA
+    return [dma((nz,)), dma((nz,)), dma((nz,)), dma((nz,)), dma((2 * nz,)), dma((2 * nz,)), dma]
+
+
+def front_kernel(
+    ny, nt, group_size, hidden, kv, w_out, whole, blocks, w_mate,
+    zs, zr, ys, yr, ms, mr, ls, ks, kr, fs, fr, ws, wr, bs,
+):
+    at = Place(ny, nt)
+    nz = at.nz
+    others = []
+    for dz in range(nz):
+        for dp in range(2):
+            if dz + dp > 0:
+                q = lax.rem(at.p + dp, 2)
+                others.append({"pool": q, "tensor": at.chip(at.up(at.z, dz), at.y)})
+    meet(others + ([at.across] if ny == 2 else []))
+
+    width = hidden.shape[1]
+    ring, from_across, finish = gather_columns(
+        at, hidden, whole, width, (zs, zr, ys, yr, ms, mr, ls)
+    )
+    ring(0)
+    me = at.rank(at.p, at.t)
+
+    def head_of(p, t):
+        return at.rank(p, t) // group_size
+
+    keep = pltpu.make_async_copy(kv.at[:, head_of(at.p, at.t)], blocks.at[me], bs)
+    keep.start()
+    half = w_mate.shape[1]
+    swap = remote(
+        w_out.at[:, pl.ds(pl.multiple_of((1 - at.p) * half, half), half)],
+        w_mate, ws, wr, at.mate,
+    )
+    sends = []
+    index = 0
+    for dz in range(nz):
+        for dp in range(2):
+            if dz + dp > 0:
+                device = others[index]
+                index += 1
+                slot = dz * 2 + dp
+                head = head_of(device["pool"], device["tensor"])
+                sends.append(remote(kv.at[:, head], blocks.at[me], ks.at[slot], kr.at[slot], device))
+                sends[-1].start()
+    swap.start()
+
+    def block_from(dz, dp):
+        return at.rank(lax.rem(at.p + dp, 2), at.chip(at.down(at.z, dz), at.y))
+
+    def forward(dz):
+        for dp in range(2):
+            slot = dz * 2 + dp
+            here = blocks.at[block_from(dz, dp)]
+            src = here
+            if slot == 0:
+                src = kv.at[:, head_of(at.p, at.t)]
+            else:
+                remote(here, here, ks.at[slot], kr.at[slot], at.mate).wait_recv()
+            if ny == 2:
+                sends.append(remote(src, here, fs.at[slot], fr.at[slot], at.across))
+                sends[-1].start()
+
+    forward(0)
+    for s in range(1, nz):
+        ring(s)
+        from_across(s - 1)
+        forward(s)
+    from_across(nz - 1)
+    finish()
+    if ny == 2:
+        for dz in range(nz):
+            for dp in range(2):
+                slot = dz * 2 + dp
+                source = at.rank(
+                    lax.rem(at.p + dp, 2), at.chip(at.down(at.z, dz), 1 - at.y)
+                )
+                there = blocks.at[source]
+                remote(there, there, fs.at[slot], fr.at[slot], at.across).wait_recv()
+    for copy in sends:
+        copy.wait_send()
+    swap.wait()
+    keep.wait()
+
+
+def front(ny, nt, group_size, hidden, kv_pool, w_out):
+    rows, width = hidden.shape
+    nz = nt // ny
+    dma = pltpu.SemaphoreType.DMA
+    blocks = (2 * nt, kv_pool.shape[0]) + kv_pool.shape[2:]
+    return pl.pallas_call(
+        functools.partial(front_kernel, ny, nt, group_size),
+        out_shape=(
+            jax.ShapeDtypeStruct((rows, width * 2 * nt), hidden.dtype),
+            jax.ShapeDtypeStruct(blocks, kv_pool.dtype),
+            jax.ShapeDtypeStruct((w_out.shape[0], w_out.shape[1] // 2), w_out.dtype),
+        ),
+        in_specs=[pl.BlockSpec(memory_space=pl.ANY)] * 3,
+        out_specs=(pl.BlockSpec(memory_space=pl.ANY),) * 3,
+        scratch_shapes=gather_sems(ny, nz)
+        + [dma((2 * nz,)), dma((2 * nz,)), dma((2 * nz,)), dma((2 * nz,)), dma, dma, dma],
+        compiler_params=pltpu.CompilerParams(
+            collective_id=0, has_side_effects=True, vmem_limit_bytes=VMEM_LIMIT
+        ),
+        name="front",
+    )(hidden, kv_pool, w_out)
+
+
+def back_kernel(
+    ny, nt, heads, w_own, w_mate, out,
+    heads_mate, w_buf, y_send, y_recv, z_send, z_recv, final,
+    hs, hr, w_sem, ps, pr, qs, qr, zs, zr, ys, yr, ms, mr, ls,
+):
+    at = Place(ny, nt)
+    nz = at.nz
+    width = final.shape[1]
+    half = w_mate.shape[1]
+
+    def load(which, t):
+        if which == 0:
+            start = pl.multiple_of(at.p * half + t * width, width)
+            src = w_own.at[:, pl.ds(start, width)]
+        else:
+            src = w_mate.at[:, pl.ds(pl.multiple_of(t * width, width), width)]
+        return pltpu.make_async_copy(src, w_buf.at[which, t], w_sem.at[which, t])
+
+    def chunk(s):
+        return at.down(at.z, s + 1)
+
+    def chip_of(s, y):
+        return at.chip(lax.rem(at.z + 2 * nz - 1 - s, nz), y)
+
+    def start_loads(y):
+        def body(s, carry):
+            t = chip_of(s, y)
+            load(0, t).start()
+            load(1, t).start()
+            return carry
+
+        lax.fori_loop(0, nz, body, 0)
+
+    if ny == 2:
+        start_loads(1 - at.y)
+    start_loads(at.y)
+    neighbours = [at.mate, at.next, at.previous] + ([at.across] if ny == 2 else [])
+    meet(neighbours)
+    trade = remote(heads, heads_mate, hs, hr, at.mate)
+    trade.start()
+    trade.wait()
+
+    def term(t):
+        load(0, t).wait()
+        load(1, t).wait()
+        return jnp.dot(heads[...], w_buf[0, t], preferred_element_type=jnp.float32) + jnp.dot(
+            heads_mate[...], w_buf[1, t], preferred_element_type=jnp.float32
+        )
+
+    def across_copy(s):
+        return remote(y_send.at[s], y_recv.at[s], ps.at[s], pr.at[s], at.across)
+
+    def ring_copy(s):
+        return remote(z_send.at[s], z_recv.at[s], qs.at[s], qr.at[s], at.next)
+
+    if ny == 2:
+
+        def send_across(s, carry):
+            y_send[s] = term(chip_of(s, 1 - at.y))
+            across_copy(s).start()
+            return carry
+
+        lax.fori_loop(0, nz, send_across, 0)
+
+    def total(s):
+        value = term(chip_of(s, at.y))
+        if ny == 2:
+            across_copy(s).wait_recv()
+            value = value + y_recv[s]
+        return value
+
+    z_send[0] = total(0)
+    ring_copy(0).start()
+
+    def ring_step(s, carry):
+        value = total(s)
+        ring_copy(s - 1).wait_recv()
+        z_send[s] = value + z_recv[s - 1]
+        ring_copy(s).start()
+        return carry
+
+    lax.fori_loop(1, nz - 1, ring_step, 0)
+    value = total(nz - 1)
+    ring_copy(nz - 2).wait_recv()
+    final[...] = (value + z_recv[nz - 2]).astype(final.dtype)
+
+    ring, from_across, finish = gather_columns(
+        at, final, out, width, (zs, zr, ys, yr, ms, mr, ls)
+    )
+    ring(0)
+    for s in range(1, nz):
+        ring(s)
+        from_across(s - 1)
+    from_across(nz - 1)
+    finish()
+
+    def sent(s, carry):
+        if ny == 2:
+            across_copy(s).wait_send()
+        return carry
+
+    lax.fori_loop(0, nz, sent, 0)
+
+    def ring_sent(s, carry):
+        ring_copy(s).wait_send()
+        return carry
+
+    lax.fori_loop(0, nz - 1, ring_sent, 0)
+
+
+def back(ny, nt, heads, w_out, w_mate):
+    rows, depth = heads.shape
+    columns = w_out.shape[1]
+    nz = nt // ny
+    width = columns // (2 * nt)
+    dma = pltpu.SemaphoreType.DMA
+    f32 = jnp.float32
+    return pl.pallas_call(
+        functools.partial(back_kernel, ny, nt),
+        out_shape=jax.ShapeDtypeStruct((rows, columns), jnp.bfloat16),
+        in_specs=[
+            pl.BlockSpec(memory_space=pltpu.VMEM),
+            pl.BlockSpec(memory_space=pl.ANY),
+            pl.BlockSpec(memory_space=pl.ANY),
+        ],
+        out_specs=pl.BlockSpec(memory_space=pl.ANY),
+        scratch_shapes=[
+            pltpu.VMEM((rows, depth), heads.dtype),
+            pltpu.VMEM((2, nt, depth, width), w_out.dtype),
+            pltpu.VMEM((nz, rows, width), f32),
+            pltpu.VMEM((nz, rows, width), f32),
+            pltpu.VMEM((nz - 1, rows, width), f32),
+            pltpu.VMEM((nz - 1, rows, width), f32),
+            pltpu.VMEM((rows, width), jnp.bfloat16),
+            dma,
+            dma,
+            dma((2, nt)),
+            dma((nz,)),
+            dma((nz,)),
+            dma((nz,)),
+            dma((nz,)),
+        ]
+        + gather_sems(ny, nz),
+        compiler_params=pltpu.CompilerParams(
+            collective_id=1, has_side_effects=True, vmem_limit_bytes=VMEM_LIMIT
+        ),
+        name="back",
+    )(heads, w_out, w_mate)
+
+
 def shards(
     hidden, norm_gain, w_query, w_out, kv_pool, draft_kv, block_table, cached_len, draft_pos
 ):
+    nt = lax.axis_size("tensor")
+    ny = 2 if nt == 8 else 1
     devices = lax.axis_size(("pool", "tensor"))
     my_rank = lax.axis_index(("pool", "tensor"))
-    block_count = kv_pool.shape[0]
     kv_heads = kv_pool.shape[1]
     block_len = kv_pool.shape[3]
     head_dim = kv_pool.shape[4]
@@ -37,7 +408,8 @@
     local_heads = w_query.shape[1] // head_dim
     group_size = devices // kv_heads
     own_head = my_rank // group_size
-    whole = lax.all_gather(hidden, ("pool", "tensor"), axis=1, tiled=True).astype(jnp.float32)
+    gathered, arrived, w_mate = front(ny, nt, group_size, hidden, kv_pool, w_out)
+    whole = gathered.astype(jnp.float32)
     normed_rows = (
         whole * lax.rsqrt(jnp.mean(whole * whole, axis=-1, keepdims=True) + 1e-05) * norm_gain
     ).astype(jnp.bfloat16)
@@ -47,8 +419,6 @@
         rotate(raw_queries.reshape(-1, local_heads, head_dim), positions) * head_dim ** (-0.5)
     ).astype(jnp.bfloat16)
     query_heads = query_heads.reshape(requests, drafts, local_heads, head_dim)
-    owner_rank = block_table // block_count
-    local_slot = block_table % block_count
     own_draft = lax.dynamic_slice_in_dim(draft_kv, own_head * head_dim, head_dim, axis=2)
     own_draft = own_draft.reshape(requests, drafts, 2, head_dim)
     draft_keys = own_draft[:, :, 0]
@@ -56,16 +426,8 @@
     draft_valid = (draft_pos[:, None, :] < draft_pos[:, :, None]) | jnp.eye(drafts, dtype=bool)[
         None
     ]
-    send_blocks = jnp.broadcast_to(
-        kv_pool[:, :, None], (block_count, kv_heads, group_size, 2, block_len, head_dim)
-    )
-    send_blocks = send_blocks.reshape(block_count, devices, 2, block_len, head_dim)
-    arrived = lax.all_to_all(
-        send_blocks, ("pool", "tensor"), split_axis=1, concat_axis=1, tiled=True
-    )
-    slot_index = local_slot * devices + owner_rank
     arrived = arrived.reshape(-1, 2, block_len, head_dim)
-    gathered_blocks = arrived[slot_index]
+    gathered_blocks = arrived[block_table]
     cache_keys = gathered_blocks[:, :, 0].reshape(requests, context, head_dim)
     cache_values = gathered_blocks[:, :, 1].reshape(requests, context, head_dim)
     cache_scores = jnp.einsum(
@@ -94,9 +456,7 @@
         "rqhp,rpd->rqhd", draft_probs, draft_values, preferred_element_type=jnp.float32
     )
     heads_out = head_rows.astype(jnp.bfloat16).reshape(requests * drafts, local_heads * head_dim)
-    partial_out = jnp.dot(heads_out, w_out, preferred_element_type=jnp.float32)
-    result = lax.psum(partial_out, ("pool", "tensor")).astype(jnp.bfloat16)
-    return result
+    return back(ny, nt, heads_out, w_out, w_mate)
 
 
 def solution(mesh):

time: 664 us -> 229 us (0.34)
  blocking collectives: 522 us -> 0 us
  Pallas kernels: 0 us -> 191 us
  waiting for transfers between devices: 81 us -> 0 us
  between operations: 13.7 us -> 0.2 us
  starting transfers between devices: 7.47 us -> 0 us
    psum x1 -> x0, blocking collectives: 522 us -> none  [shards(): result = lax.psum(partial_out, ('pool', 'tensor')).astype(jnp.bfloat16)]
    pallas_call x0 -> x2, Pallas kernels: none -> 191 us  [the longest x1 119 us: back(): pl.pallas_call(functools.partial(back_kernel, ny, nt), out_shape=jax.Shap...]
    all_to_all x1 -> x0, waiting for transfers between devices: 80.3 us -> none  [shards(): lax.all_to_all(send_blocks, ('pool', 'tensor'), split_axis=1, concat_axis...]
    all_to_all x1 -> x0, starting transfers between devices: 7.44 us -> none  [shards(): lax.all_to_all(send_blocks, ('pool', 'tensor'), split_axis=1, concat_axis...]
    unnamed x21 -> x16, local copies, waits for them, and re-layouts: 1.66 us -> 8.75 us
  transfers between devices with their start and end apart: 2 -> 0, of which waited for: 1 -> 0; matrix products, arithmetic and copies ran while one was open for 2% -> 0% of each run, Pallas kernels for 0% -> 0%
where the time goes in v1:
time: 229 us
  Pallas kernels  191 us (83%)
  local copies, waits for them, and re-layouts  18.4 us (8%)
  matrix products  12.4 us (5%)
  other arithmetic  6.88 us (3%)
    pallas_call x1, Pallas kernels, back(): pl.pallas_call(functools.partial(back_kernel, ny, nt), out_shape=jax.Shap...  119 us
    pallas_call x1, Pallas kernels, front(): pl.pallas_call(functools.partial(front_kernel, ny, nt, group_size), out_s...  71.7 us
    unnamed x16, local copies, waits for them, and re-layouts  8.75 us
    reshape x1, matrix products, shards(): raw_queries.reshape(-1, local_heads, head_dim)  7.66 us

profile of v1, /device:TPU:0, one launch (start us, length us, event | category | flops | bytes accessed | tf_op | source)
XLA Modules:
  0.0 228.7 jit_solution(15065505412035520571)
XLA Ops:
  0.0 1.4 copy-done
  1.5 0.7 copy.20
  2.3 71.7 %front.1 = (bf16[384,8192]{1,0:T(8,128)(2,1)}, bf16[16,2,2,128,128]{4,3,2,1,0:T(8,128)(2,1)}, bf16[512,4096]{1,0:T(8,128)(2,1)}) custom-call(bf16[384,512]{1,0:T(8,128)(2,1)} %hidden.1, bf16[2,8,2,128,128]{4,3,2,1,0:T(8,128)(2,1)} %kv.1, bf16[512,8192]{1,0:T(8,128)(2,1)} %w_own.1), custom_call_target="tpu_custom_call" | custom-call | tf_op jit(solution)/shard_map/front/pallas_call | solution.py:226
  73.9 4.3 %fusion = f32[384]{0:T(512)S(1)} fusion(bf16[384,8192]{1,0:T(8,128)(2,1)} %get-tuple-element.8), kind=kLoop, calls=%fused_computation.3 | loop fusion | flops 9436800 | bytes 6292992 | tf_op jit(solution)/shard_map/reduce_sum | solution.py:414
  78.2 0.3 copy-done.1
  78.5 7.7 %fusion.3 = f32[384,512]{0,1:T(8,128)S(1)} fusion(bf16[8192,512]{1,0:T(8,128)(2,1)} %param.11, bf16[384,8192]{1,0:T(8,128)(2,1)S(1)} %copy-done.1, f32[8192]{0:T(1024)S(1)} %copy-done.6, f32[384]{0:T(512)S(1)} %add_rsqrt_fusion), kind=kOutput, calls=%fused_computation.6 | convolution fusion | flops 3233808384 | bytes 15500800 | tf_op jit(solution)/shard_map/reshape | solution.py:419
  86.4 0.4 multiply_cosine_fusion
  86.9 0.3 concatenate.8
  87.3 0.3 copy.17
  87.6 1.1 concatenate.9
  88.7 1.3 copy.18
  90.0 0.3 fusion.10
  90.4 1.3 fusion.16
  91.9 3.7 %gather_fusion = bf16[32,2,128,128]{3,2,1,0:T(8,128)(2,1)} fusion(bf16[32,2,128,128]{3,2,1,0:T(8,128)(2,1)} %bitcast.48, s32[1024]{0:T(1024)S(1)} %pad_clamp_fusion), kind=kCustom, calls=%fused_computation | custom fusion | bytes 4194432 | tf_op jit(solution)/shard_map/gather | solution.py:430
  95.6 1.7 fusion.15
  97.4 1.1 select_reduce_fusion
  98.5 0.2 fusion.11
  98.6 1.3 fusion.7
  100.0 2.0 fusion.8
  102.0 0.3 fusion.9
  102.3 0.2 copy.23
  102.5 0.8 copy.34
  103.3 119.1 %back.1 = bf16[384,8192]{1,0:T(8,128)(2,1)} custom-call(bf16[384,512]{1,0:T(8,128)(2,1)} %bitcast.50, bf16[512,8192]{1,0:T(8,128)(2,1)} %w_own.1, bf16[512,4096]{1,0:T(8,128)(2,1)} %get-tuple-element.10.w_mate), custom_call_target="tpu_custom_call" | custom-call | tf_op jit(solution)/shard_map/back/pallas_call | solution.py:361
  222.5 6.2 %copy.36 = bf16[384,8192]{1,0:T(8,128)(2,1)} copy(bf16[384,8192]{1,0:T(8,128)(2,1)} %back.1) | data formatting | bytes 12582912
  (26 shorter events, 0.7 us)
Async XLA Ops:
  0.0 1.4 copy-start
  2.3 75.9 %copy-start.6 = (f32[8192]{0:T(1024)S(1)}, f32[8192]{0:T(1024)}, u32[]{:S(2)}) copy-start(f32[8192]{0:T(1024)} %param.10) | copy-start | bytes 98308
  73.9 4.6 %copy-start.1 = (bf16[384,8192]{1,0:T(8,128)(2,1)S(1)}, bf16[384,8192]{1,0:T(8,128)(2,1)}, u32[]{:S(2)}) copy-start(bf16[384,8192]{1,0:T(8,128)(2,1)} %get-tuple-element.8) | copy-start | bytes 18874372
  78.5 7.7 %copy-start.3 = (s32[4,96]{1,0:T(4,128)S(1)}, s32[4,96]{1,0:T(4,128)}, u32[]{:S(2)}) copy-start(s32[4,96]{1,0:T(4,128)} %param.17) | copy-start | bytes 4612
  78.5 7.7 %copy-start.4 = (s32[4]{0:T(128)S(1)}, s32[4]{0:T(128)}, u32[]{:S(2)}) copy-start(s32[4]{0:T(128)} %param.16) | copy-start | bytes 52
  86.2 5.6 %copy-start.5 = (s32[4,8]{1,0:T(4,128)S(1)}, s32[4,8]{1,0:T(4,128)}, u32[]{:S(2)}) copy-start(s32[4,8]{1,0:T(4,128)} %param.15) | copy-start | bytes 388
  100.0 2.0 copy-start.2

commit v2 on v1

--- a/solution.py
+++ b/solution.py
@@ -82,16 +82,17 @@
     pl.semaphore_wait(barrier, len(devices))
 
 
-def gather_columns(at, own, out, width, sems):
+def gather_blocks(at, own, block_of, sems, use=None):
     zs, zr, ys, yr, ms, mr, ls = sems
     nz, ny = at.nz, at.ny
 
     def block(p, z, y):
-        start = pl.multiple_of(at.rank(p, at.chip(z, y)) * width, width)
-        return out.at[:, pl.ds(start, width)]
-
-    keep = pltpu.make_async_copy(own, block(at.p, at.z, at.y), ls)
-    keep.start()
+        return block_of(at.rank(p, at.chip(z, y)))
+
+    keep = None
+    if use is None:
+        keep = pltpu.make_async_copy(own, block(at.p, at.z, at.y), ls)
+        keep.start()
     started = []
 
     def ring(s):
@@ -116,19 +117,25 @@
             started.append(remote(there, there, ms.at[nz + s], mr.at[nz + s], at.mate))
             started[-1].start()
 
+    def arrive(s):
+        z = at.down(at.z, s)
+        for y_at in range(ny):
+            y = at.y if y_at == 0 else 1 - at.y
+            there = block(1 - at.p, z, y)
+            slot = s + y_at * nz
+            if use is not None and s + y_at > 0:
+                use(at.rank(at.p, at.chip(z, y)))
+            remote(there, there, ms.at[slot], mr.at[slot], at.mate).wait_recv()
+            if use is not None:
+                use(at.rank(1 - at.p, at.chip(z, y)))
+
     def finish():
-        for s in range(nz):
-            z = at.down(at.z, s)
-            for y_at in range(ny):
-                y = at.y if y_at == 0 else 1 - at.y
-                there = block(1 - at.p, z, y)
-                slot = s + y_at * nz
-                remote(there, there, ms.at[slot], mr.at[slot], at.mate).wait_recv()
         for copy in started:
             copy.wait_send()
-        keep.wait()
-
-    return ring, from_across, finish
+        if keep is not None:
+            keep.wait()
+
+    return ring, from_across, arrive, finish
 
 
 def gather_sems(ny, nz):
@@ -137,25 +144,45 @@
 
 
 def front_kernel(
-    ny, nt, group_size, hidden, kv, w_out, whole, blocks, w_mate,
-    zs, zr, ys, yr, ms, mr, ls, ks, kr, fs, fr, ws, wr, bs,
+    ny, nt, group_size, hidden, gain, kv, w_out, w_query, raw, blocks, w_mate,
+    squares, squares_all, normed, gathered, w_buf,
+    zs, zr, ys, yr, ms, mr, ls, ks, kr, fs, fr, ws, wr, bs, w_sem, ss, sr,
 ):
     at = Place(ny, nt)
     nz = at.nz
+    ranks = 2 * nt
+    width = hidden.shape[1]
+
+    def load(rank):
+        start = pl.multiple_of(rank * width, width)
+        return pltpu.make_async_copy(
+            w_query.at[pl.ds(start, width), :], w_buf.at[rank], w_sem.at[rank]
+        )
+
+    def start_load(rank, carry):
+        load(rank).start()
+        return carry
+
+    lax.fori_loop(0, ranks, start_load, 0)
     others = []
-    for dz in range(nz):
+    for dt in range(nt):
         for dp in range(2):
-            if dz + dp > 0:
-                q = lax.rem(at.p + dp, 2)
-                others.append({"pool": q, "tensor": at.chip(at.up(at.z, dz), at.y)})
-    meet(others + ([at.across] if ny == 2 else []))
-
-    width = hidden.shape[1]
-    ring, from_across, finish = gather_columns(
-        at, hidden, whole, width, (zs, zr, ys, yr, ms, mr, ls)
-    )
-    ring(0)
+            if dt + dp > 0:
+                others.append({"pool": lax.rem(at.p + dp, 2), "tensor": lax.rem(at.t + dt, nt)})
+    meet(others)
     me = at.rank(at.p, at.t)
+
+    wide = hidden[...].astype(jnp.float32)
+    squares[...] = lax.dot_general(
+        jnp.ones((8, width), jnp.float32), wide * wide, (((1,), (1,)), ((), ())),
+        precision=lax.Precision.HIGHEST, preferred_element_type=jnp.float32,
+    )
+    square_copies = [
+        remote(squares, squares_all.at[i], ss.at[i], sr.at[i], device)
+        for i, device in enumerate(others)
+    ]
+    for copy in square_copies:
+        copy.start()
 
     def head_of(p, t):
         return at.rank(p, t) // group_size
@@ -168,17 +195,37 @@
         w_mate, ws, wr, at.mate,
     )
     sends = []
-    index = 0
     for dz in range(nz):
         for dp in range(2):
             if dz + dp > 0:
-                device = others[index]
-                index += 1
+                device = {
+                    "pool": lax.rem(at.p + dp, 2),
+                    "tensor": at.chip(at.up(at.z, dz), at.y),
+                }
                 slot = dz * 2 + dp
                 head = head_of(device["pool"], device["tensor"])
                 sends.append(remote(kv.at[:, head], blocks.at[me], ks.at[slot], kr.at[slot], device))
                 sends[-1].start()
-    swap.start()
+
+    total = squares[...]
+    for i, copy in enumerate(square_copies):
+        copy.wait_recv()
+        total = total + squares_all[i]
+    scale = lax.rsqrt(total * (1.0 / (width * ranks)) + 1e-05)
+    scale = jnp.transpose(jnp.concatenate([scale] * 16, axis=0))
+    for c in range(width // 128):
+        lanes = slice(c * 128, (c + 1) * 128)
+        normed[:, lanes] = (
+            hidden[:, lanes].astype(jnp.float32) * scale * gain[:, lanes]
+        ).astype(normed.dtype)
+
+    def use(rank):
+        load(rank).wait()
+        raw[...] += jnp.dot(gathered[rank], w_buf[rank], preferred_element_type=jnp.float32)
+
+    ring, from_across, arrive, finish = gather_blocks(
+        at, normed, lambda rank: gathered.at[rank], (zs, zr, ys, yr, ms, mr, ls), use
+    )
 
     def block_from(dz, dp):
         return at.rank(lax.rem(at.p + dp, 2), at.chip(at.down(at.z, dz), at.y))
@@ -196,12 +243,18 @@
                 sends.append(remote(src, here, fs.at[slot], fr.at[slot], at.across))
                 sends[-1].start()
 
+    ring(0)
     forward(0)
+    swap.start()
+    load(me).wait()
+    raw[...] = jnp.dot(normed[...], w_buf[me], preferred_element_type=jnp.float32)
     for s in range(1, nz):
         ring(s)
         from_across(s - 1)
         forward(s)
+        arrive(s - 1)
     from_across(nz - 1)
+    arrive(nz - 1)
     finish()
     if ny == 2:
         for dz in range(nz):
@@ -212,39 +265,65 @@
                 )
                 there = blocks.at[source]
                 remote(there, there, fs.at[slot], fr.at[slot], at.across).wait_recv()
-    for copy in sends:
+    for copy in sends + square_copies:
         copy.wait_send()
     swap.wait()
     keep.wait()
 
 
-def front(ny, nt, group_size, hidden, kv_pool, w_out):
+def front(ny, nt, group_size, hidden, gain, kv_pool, w_out, w_query):
     rows, width = hidden.shape
+    columns = w_query.shape[1]
     nz = nt // ny
+    ranks = 2 * nt
     dma = pltpu.SemaphoreType.DMA
-    blocks = (2 * nt, kv_pool.shape[0]) + kv_pool.shape[2:]
+    blocks = (ranks, kv_pool.shape[0]) + kv_pool.shape[2:]
     return pl.pallas_call(
         functools.partial(front_kernel, ny, nt, group_size),
         out_shape=(
-            jax.ShapeDtypeStruct((rows, width * 2 * nt), hidden.dtype),
+            jax.ShapeDtypeStruct((rows, columns), jnp.float32),
             jax.ShapeDtypeStruct(blocks, kv_pool.dtype),
             jax.ShapeDtypeStruct((w_out.shape[0], w_out.shape[1] // 2), w_out.dtype),
         ),
-        in_specs=[pl.BlockSpec(memory_space=pl.ANY)] * 3,
-        out_specs=(pl.BlockSpec(memory_space=pl.ANY),) * 3,
-        scratch_shapes=gather_sems(ny, nz)
-        + [dma((2 * nz,)), dma((2 * nz,)), dma((2 * nz,)), dma((2 * nz,)), dma, dma, dma],
+        in_specs=[pl.BlockSpec(memory_space=pltpu.VMEM)] * 2
+        + [pl.BlockSpec(memory_space=pl.ANY)] * 3,
+        out_specs=(
+            pl.BlockSpec(memory_space=pltpu.VMEM),
+            pl.BlockSpec(memory_space=pl.ANY),
+            pl.BlockSpec(memory_space=pl.ANY),
+        ),
+        scratch_shapes=[
+            pltpu.VMEM((8, rows), jnp.float32),
+            pltpu.VMEM((ranks - 1, 8, rows), jnp.float32),
+            pltpu.VMEM((rows, width), hidden.dtype),
+            pltpu.VMEM((ranks, rows, width), hidden.dtype),
+            pltpu.VMEM((ranks, width, columns), w_query.dtype),
+        ]
+        + gather_sems(ny, nz)
+        + [dma((2 * nz,)), dma((2 * nz,)), dma((2 * nz,)), dma((2 * nz,)), dma, dma, dma]
+        + [dma((ranks,)), dma((ranks - 1,)), dma((ranks - 1,))],
         compiler_params=pltpu.CompilerParams(
             collective_id=0, has_side_effects=True, vmem_limit_bytes=VMEM_LIMIT
         ),
         name="front",
-    )(hidden, kv_pool, w_out)
+    )(hidden, gain, kv_pool, w_out, w_query)
+
+
+def code(value, codes, scales):
+    peak = jnp.maximum(jnp.max(jnp.abs(value), axis=0, keepdims=True), 1e-30)
+    codes[...] = jnp.round(value * (32767.0 / peak)).astype(jnp.int32).astype(jnp.int16)
+    scales[...] = jnp.broadcast_to(peak * (1.0 / 32767.0), scales.shape)
+
+
+def decode(codes, scales):
+    return codes[...].astype(jnp.int32).astype(jnp.float32) * scales[0:1, :]
 
 
 def back_kernel(
     ny, nt, heads, w_own, w_mate, out,
-    heads_mate, w_buf, y_send, y_recv, z_send, z_recv, final,
-    hs, hr, w_sem, ps, pr, qs, qr, zs, zr, ys, yr, ms, mr, ls,
+    heads_mate, w_buf, y_send, y_recv, z_send, z_recv,
+    y_send_scale, y_recv_scale, z_send_scale, z_recv_scale, final,
+    hs, hr, w_sem, ps, pr, qs, qr, pss, psr, qss, qsr, zs, zr, ys, yr, ms, mr, ls,
 ):
     at = Place(ny, nt)
     nz = at.nz
@@ -290,17 +369,24 @@
             heads_mate[...], w_buf[1, t], preferred_element_type=jnp.float32
         )
 
-    def across_copy(s):
-        return remote(y_send.at[s], y_recv.at[s], ps.at[s], pr.at[s], at.across)
-
-    def ring_copy(s):
-        return remote(z_send.at[s], z_recv.at[s], qs.at[s], qr.at[s], at.next)
+    def across_copies(s):
+        return [
+            remote(y_send.at[s], y_recv.at[s], ps.at[s], pr.at[s], at.across),
+            remote(y_send_scale.at[s], y_recv_scale.at[s], pss.at[s], psr.at[s], at.across),
+        ]
+
+    def ring_copies(s):
+        return [
+            remote(z_send.at[s], z_recv.at[s], qs.at[s], qr.at[s], at.next),
+            remote(z_send_scale.at[s], z_recv_scale.at[s], qss.at[s], qsr.at[s], at.next),
+        ]
 
     if ny == 2:
 
         def send_across(s, carry):
-            y_send[s] = term(chip_of(s, 1 - at.y))
-            across_copy(s).start()
+            code(term(chip_of(s, 1 - at.y)), y_send.at[s], y_send_scale.at[s])
+            for copy in across_copies(s):
+                copy.start()
             return carry
 
         lax.fori_loop(0, nz, send_across, 0)
@@ -308,44 +394,58 @@
     def total(s):
         value = term(chip_of(s, at.y))
         if ny == 2:
-            across_copy(s).wait_recv()
-            value = value + y_recv[s]
+            for copy in across_copies(s):
+                copy.wait_recv()
+            value = value + decode(y_recv.at[s], y_recv_scale.at[s])
         return value
 
-    z_send[0] = total(0)
-    ring_copy(0).start()
+    def ring_received(s):
+        for copy in ring_copies(s):
+            copy.wait_recv()
+        return decode(z_recv.at[s], z_recv_scale.at[s])
+
+    def ring_send(s, value):
+        code(value, z_send.at[s], z_send_scale.at[s])
+        for copy in ring_copies(s):
+            copy.start()
+
+    ring_send(0, total(0))
 
     def ring_step(s, carry):
         value = total(s)
-        ring_copy(s - 1).wait_recv()
-        z_send[s] = value + z_recv[s - 1]
-        ring_copy(s).start()
+        ring_send(s, value + ring_received(s - 1))
         return carry
 
     lax.fori_loop(1, nz - 1, ring_step, 0)
     value = total(nz - 1)
-    ring_copy(nz - 2).wait_recv()
-    final[...] = (value + z_recv[nz - 2]).astype(final.dtype)
-
-    ring, from_across, finish = gather_columns(
-        at, final, out, width, (zs, zr, ys, yr, ms, mr, ls)
+    final[...] = (value + ring_received(nz - 2)).astype(final.dtype)
+
+    def block_of(rank):
+        return out.at[:, pl.ds(pl.multiple_of(rank * width, width), width)]
+
+    ring, from_across, arrive, finish = gather_blocks(
+        at, final, block_of, (zs, zr, ys, yr, ms, mr, ls)
     )
     ring(0)
     for s in range(1, nz):
         ring(s)
         from_across(s - 1)
     from_across(nz - 1)
+    for s in range(nz):
+        arrive(s)
     finish()
 
     def sent(s, carry):
         if ny == 2:
-            across_copy(s).wait_send()
+            for copy in across_copies(s):
+                copy.wait_send()
         return carry
 
     lax.fori_loop(0, nz, sent, 0)
 
     def ring_sent(s, carry):
-        ring_copy(s).wait_send()
+        for copy in ring_copies(s):
+            copy.wait_send()
         return carry
 
     lax.fori_loop(0, nz - 1, ring_sent, 0)
@@ -370,14 +470,22 @@
         scratch_shapes=[
             pltpu.VMEM((rows, depth), heads.dtype),
             pltpu.VMEM((2, nt, depth, width), w_out.dtype),
-            pltpu.VMEM((nz, rows, width), f32),
-            pltpu.VMEM((nz, rows, width), f32),
-            pltpu.VMEM((nz - 1, rows, width), f32),
-            pltpu.VMEM((nz - 1, rows, width), f32),
+            pltpu.VMEM((nz, rows, width), jnp.int16),
+            pltpu.VMEM((nz, rows, width), jnp.int16),
+            pltpu.VMEM((nz - 1, rows, width), jnp.int16),
+            pltpu.VMEM((nz - 1, rows, width), jnp.int16),
+            pltpu.VMEM((nz, 8, width), f32),
+            pltpu.VMEM((nz, 8, width), f32),
+            pltpu.VMEM((nz - 1, 8, width), f32),
+            pltpu.VMEM((nz - 1, 8, width), f32),
             pltpu.VMEM((rows, width), jnp.bfloat16),
             dma,
             dma,
             dma((2, nt)),
+            dma((nz,)),
+            dma((nz,)),
+            dma((nz,)),
+            dma((nz,)),
             dma((nz,)),
             dma((nz,)),
             dma((nz,)),
@@ -408,12 +516,11 @@
     local_heads = w_query.shape[1] // head_dim
     group_size = devices // kv_heads
     own_head = my_rank // group_size
-    gathered, arrived, w_mate = front(ny, nt, group_size, hidden, kv_pool, w_out)
-    whole = gathered.astype(jnp.float32)
-    normed_rows = (
-        whole * lax.rsqrt(jnp.mean(whole * whole, axis=-1, keepdims=True) + 1e-05) * norm_gain
-    ).astype(jnp.bfloat16)
-    raw_queries = jnp.dot(normed_rows, w_query, preferred_element_type=jnp.float32)
+    width = hidden.shape[1]
+    gain = lax.dynamic_slice_in_dim(norm_gain, my_rank * width, width).reshape(1, width)
+    raw_queries, arrived, w_mate = front(
+        ny, nt, group_size, hidden, gain, kv_pool, w_out, w_query
+    )
     positions = (cached_len[:, None] + draft_pos).reshape(-1)
     query_heads = (
         rotate(raw_queries.reshape(-1, local_heads, head_dim), positions) * head_dim ** (-0.5)

time: 229 us -> 209 us (0.913)
  Pallas kernels: 191 us -> 172 us
  matrix products: 12.4 us -> 6.44 us
  local copies, waits for them, and re-layouts: 18.4 us -> 21.9 us
    pallas_call x1, Pallas kernels: 119 us -> 88.5 us  [back(): pl.pallas_call(functools.partial(back_kernel, ny, nt), out_shape=jax.Shap...]
    pallas_call x1, Pallas kernels: 71.7 us -> 83.3 us  [front(): pl.pallas_call(functools.partial(front_kernel, ny, nt, group_size), out_s...]
    reshape x1 -> x0, matrix products: 7.66 us -> none  [shards(): raw_queries.reshape(-1, local_heads, head_dim)]
    reduce_sum x1 -> x0, other arithmetic: 4.25 us -> none  [shards(): jnp.mean(whole * whole, axis=-1, keepdims=True) + 1e-05]
    reduce_sum x1, other arithmetic: 1.35 us -> 4.4 us  [shards(): jnp.sum(cache_weights, axis=-1, keepdims=True)]
    dot_general x1, matrix products: 1.08 us -> 3.69 us  [shards(): jnp.einsum('rqhd,rkd->rqhk', query_heads, cache_keys, preferred_element_t...]
    unnamed x16 -> x14, local copies, waits for them, and re-layouts: 8.75 us -> 7.03 us
where the time goes in v2:
time: 209 us; the launch traced here: 208 us
  Pallas kernels  172 us (82%)
  local copies, waits for them, and re-layouts  21.9 us (10%)
  other arithmetic  7.91 us (4%)
  matrix products  6.44 us (3%)
    pallas_call x1, Pallas kernels, back(): pl.pallas_call(functools.partial(back_kernel, ny, nt), out_shape=jax.Shap...  88.5 us
    pallas_call x1, Pallas kernels, front(): pl.pallas_call(functools.partial(front_kernel, ny, nt, group_size), out_s...  83.3 us
    unnamed x14, local copies, waits for them, and re-layouts  7.03 us
    concatenate x4, local copies, waits for them, and re-layouts, rotate(): jnp.concatenate([first_half * cosine - second_half * sine_part, second_ha...  5.01 us
    reduce_sum x1, other arithmetic, shards(): jnp.sum(cache_weights, axis=-1, keepdims=True)  4.4 us

profile of v2, /device:TPU:0, one launch (start us, length us, event | category | flops | bytes accessed | tf_op | source)
XLA Modules:
  0.0 208.1 jit_solution(6308091605712843843)
XLA Ops:
  0.0 1.5 dynamic_slice.6
  1.5 83.3 %front.1 = (f32[384,512]{1,0:T(8,128)}, bf16[16,2,2,128,128]{4,3,2,1,0:T(8,128)(2,1)}, bf16[512,4096]{1,0:T(8,128)(2,1)}) custom-call(bf16[384,512]{1,0:T(8,128)(2,1)} %hidden.1, f32[1,512]{1,0:T(1,128)} %bitcast.55, bf16[2,8,2,128,128]{4,3,2,1,0:T(8,128)(2,1)} %kv.1, bf16[512,8192]{1,0:T(8,128)(2,1)} %w_own.1, bf16[8192,512]{1,0:T(8,128)(2,1)} %w_query.1), custom_call_target="tpu_custom_call" | custom-call | tf_op jit(solution)/shard_map/front/pallas_call | solution.py:281
  84.9 3.7 %gather_fusion = bf16[32,2,128,128]{3,2,1,0:T(8,128)(2,1)} fusion(bf16[32,2,128,128]{3,2,1,0:T(8,128)(2,1)} %bitcast.49, s32[1024]{0:T(1024)S(1)} %pad_clamp_fusion), kind=kCustom, calls=%fused_computation | custom fusion | bytes 4194432 | tf_op jit(solution)/shard_map/gather | solution.py:537
  88.6 2.7 %fusion.8 = (bf16[4,8,1,128,128]{4,3,2,1,0:T(8,128)(2,1)S(1)}, bf16[4,8,1,128,128]{4,3,2,1,0:T(8,128)(2,1)}) fusion(bf16[4,8,2,128,128]{4,3,2,1,0:T(8,128)(2,1)} %bitcast.46), kind=kLoop, calls=%fused_computation.32 | loop fusion | bytes 4194304 | tf_op jit(solution)/shard_map/slice | solution.py:538
  91.4 1.4 copy.29
  93.0 0.4 multiply_cosine_fusion
  93.4 1.0 multiply_subtract_fusion
  94.4 1.3 concatenate.9
  95.7 1.2 copy.18
  96.9 1.3 concatenate.8
  98.2 1.2 copy.17
  99.4 1.6 fusion.3
  101.0 3.7 %select_reduce_fusion = (f32[4,96,4]{1,2,0:T(4,128)S(1)}, f32[4,96,4,1024]{3,1,2,0:T(8,128)}) fusion(pred[4,1024]{1,0:T(4,128)(4,1)S(1)} %iota_compare_fusion.1, bf16[4,96,4,128]{3,1,2,0:T(8,128)(2,1)S(1)} %fusion.3, bf16[4,1024,128,1]{2,1,3,0:T(8,128)(2,1)S(1)} %bitcast.47), kind=kOutput, calls=%fused_computation.3 | convolution fusion | flops 405797376 | bytes 7743488 | tf_op jit(solution)/shard_map/rqhd,rkd->rqhk/dot_general | solution.py:540
  104.7 0.1 constant_dynamic-slice_fusion
  105.0 0.1 compare_or_fusion
  105.1 0.4 fusion.9
  105.5 4.4 %fusion = f32[4,96,4]{1,2,0:T(4,128)S(1)} fusion(f32[4,96,4,1024]{3,1,2,0:T(8,128)} %get-tuple-element.18, f32[4,96,4]{1,2,0:T(4,128)S(1)} %max.8, pred[4,1024]{1,0:T(4,128)(4,1)S(1)} %iota_compare_fusion.1), kind=kLoop, calls=%fused_computation.4 | loop fusion | flops 4717056 | bytes 6307840 | tf_op jit(solution)/shard_map/reduce_sum | solution.py:554
  109.9 0.2 fusion.4
  110.1 2.0 fusion.1
  112.1 0.3 fusion.2
  112.5 0.2 copy.23
  112.7 0.8 copy.34
  113.5 88.5 %back.1 = bf16[384,8192]{1,0:T(8,128)(2,1)} custom-call(bf16[384,512]{1,0:T(8,128)(2,1)} %bitcast.51, bf16[512,8192]{1,0:T(8,128)(2,1)} %w_own.1, bf16[512,4096]{1,0:T(8,128)(2,1)} %get-tuple-element.10.w_mate), custom_call_target="tpu_custom_call" | custom-call | tf_op jit(solution)/shard_map/back/pallas_call | solution.py:461
  201.9 6.2 %copy.36 = bf16[384,8192]{1,0:T(8,128)(2,1)} copy(bf16[384,8192]{1,0:T(8,128)(2,1)} %back.1) | data formatting | bytes 12582912
  (23 shorter events, 0.4 us)
Async XLA Ops:
  0.0 104.7 %copy-start = (bf16[384,2,1024]{2,1,0:T(2,128)(2,1)S(1)}, bf16[384,2,1024]{2,1,0:T(2,128)(2,1)}, u32[]{:S(2)}) copy-start(bf16[384,2,1024]{2,1,0:T(2,128)(2,1)} %param.14) | copy-start | bytes 4718596
  1.5 83.3 %copy-start.5 = (s32[4,8]{1,0:T(4,128)S(1)}, s32[4,8]{1,0:T(4,128)}, u32[]{:S(2)}) copy-start(s32[4,8]{1,0:T(4,128)} %param.15) | copy-start | bytes 388
  84.7 6.6 %copy-start.4 = (s32[4]{0:T(128)S(1)}, s32[4]{0:T(128)}, u32[]{:S(2)}) copy-start(s32[4]{0:T(128)} %param.16) | copy-start | bytes 52
  84.7 8.1 %copy-start.3 = (s32[4,96]{1,0:T(4,128)S(1)}, s32[4,96]{1,0:T(4,128)}, u32[]{:S(2)}) copy-start(s32[4,96]{1,0:T(4,128)} %param.17) | copy-start | bytes 4612
  104.7 5.4 %copy-start.2 = (bf16[4,8,1,128,128]{4,3,2,1,0:T(8,128)(2,1)S(1)}, bf16[4,8,1,128,128]{4,3,2,1,0:T(8,128)(2,1)}, u32[]{:S(2)}) copy-start(bf16[4,8,1,128,128]{4,3,2,1,0:T(8,128)(2,1)} %get-tuple-element.12) | copy-start | bytes 3145732
  104.7 5.4 %copy-start.1 = (f32[4,96,4,1024]{3,1,2,0:T(8,128)S(1)}, f32[4,96,4,1024]{3,1,2,0:T(8,128)}, u32[]{:S(2)}) copy-start(f32[4,96,4,1024]{3,1,2,0:T(8,128)} %get-tuple-element.18) | copy-start | bytes 18874372

commit v3 on v2

--- a/solution.py
+++ b/solution.py
@@ -8,23 +8,7 @@
 from jax.sharding import PartitionSpec as P
 
 VMEM_LIMIT = 56 * 1024 * 1024
-
-
-def rotate(values, positions):
-    half_dim = values.shape[-1] // 2
-    frequency = 500000.0 ** (-(jnp.arange(half_dim, dtype=jnp.float32) * 2.0) / values.shape[-1])
-    angles = positions.astype(jnp.float32)[:, None] * frequency[None, :]
-    cosine = jnp.cos(angles)[:, None, :]
-    sine_part = jnp.sin(angles)[:, None, :]
-    first_half = values[..., :half_dim]
-    second_half = values[..., half_dim:]
-    return jnp.concatenate(
-        [
-            first_half * cosine - second_half * sine_part,
-            second_half * cosine + first_half * sine_part,
-        ],
-        axis=-1,
-    )
+PIECES = 2
 
 
 class Place:
@@ -85,47 +69,59 @@
 def gather_blocks(at, own, block_of, sems, use=None):
     zs, zr, ys, yr, ms, mr, ls = sems
     nz, ny = at.nz, at.ny
-
-    def block(p, z, y):
-        return block_of(at.rank(p, at.chip(z, y)))
+    part = own.shape[0] // PIECES
+
+    def rows(ref, h):
+        return ref.at[pl.ds(h * part, part), :]
+
+    def block(p, z, y, h):
+        return rows(block_of(at.rank(p, at.chip(z, y))), h)
 
     keep = None
     if use is None:
-        keep = pltpu.make_async_copy(own, block(at.p, at.z, at.y), ls)
+        keep = pltpu.make_async_copy(own, block_of(at.rank(at.p, at.t)), ls)
         keep.start()
     started = []
 
-    def ring(s):
+    def send(src, dst, send_sem, recv_sem, device):
+        started.append(remote(src, dst, send_sem, recv_sem, device))
+        started[-1].start()
+
+    def ring(s, h):
         z = at.down(at.z, s)
-        here = block(at.p, z, at.y)
-        src = own if s == 0 else here
+        here = block(at.p, z, at.y, h)
+        src = rows(own, h) if s == 0 else here
         if s > 0:
-            remote(here, here, zs.at[s - 1], zr.at[s - 1], at.previous).wait_recv()
+            remote(here, here, zs.at[s - 1, h], zr.at[s - 1, h], at.previous).wait_recv()
         if s < nz - 1:
-            started.append(remote(src, here, zs.at[s], zr.at[s], at.next))
-            started[-1].start()
+            send(src, here, zs.at[s, h], zr.at[s, h], at.next)
         if ny == 2:
-            started.append(remote(src, here, ys.at[s], yr.at[s], at.across))
-            started[-1].start()
-        started.append(remote(src, here, ms.at[s], mr.at[s], at.mate))
-        started[-1].start()
-
-    def from_across(s):
+            send(src, here, ys.at[s, h], yr.at[s, h], at.across)
+        send(src, here, ms.at[s, h], mr.at[s, h], at.mate)
+
+    def from_across(s, h):
         if ny == 2:
-            there = block(at.p, at.down(at.z, s), 1 - at.y)
-            remote(there, there, ys.at[s], yr.at[s], at.across).wait_recv()
-            started.append(remote(there, there, ms.at[nz + s], mr.at[nz + s], at.mate))
-            started[-1].start()
+            there = block(at.p, at.down(at.z, s), 1 - at.y, h)
+            remote(there, there, ys.at[s, h], yr.at[s, h], at.across).wait_recv()
+            send(there, there, ms.at[nz + s, h], mr.at[nz + s, h], at.mate)
+
+    def step(s):
+        for h in range(PIECES):
+            if s < nz:
+                ring(s, h)
+            if s > 0:
+                from_across(s - 1, h)
 
     def arrive(s):
         z = at.down(at.z, s)
         for y_at in range(ny):
             y = at.y if y_at == 0 else 1 - at.y
-            there = block(1 - at.p, z, y)
             slot = s + y_at * nz
             if use is not None and s + y_at > 0:
                 use(at.rank(at.p, at.chip(z, y)))
-            remote(there, there, ms.at[slot], mr.at[slot], at.mate).wait_recv()
+            for h in range(PIECES):
+                there = block(1 - at.p, z, y, h)
+                remote(there, there, ms.at[slot, h], mr.at[slot, h], at.mate).wait_recv()
             if use is not None:
                 use(at.rank(1 - at.p, at.chip(z, y)))
 
@@ -135,17 +131,18 @@
         if keep is not None:
             keep.wait()
 
-    return ring, from_across, arrive, finish
+    return step, arrive, finish
 
 
 def gather_sems(ny, nz):
     dma = pltpu.SemaphoreType.DMA
-    return [dma((nz,)), dma((nz,)), dma((nz,)), dma((nz,)), dma((2 * nz,)), dma((2 * nz,)), dma]
+    once, twice = dma((nz, PIECES)), dma((2 * nz, PIECES))
+    return [once, once, once, once, twice, twice, dma]
 
 
 def front_kernel(
     ny, nt, group_size, hidden, gain, kv, w_out, w_query, raw, blocks, w_mate,
-    squares, squares_all, normed, gathered, w_buf,
+    squares, squares_all, scales, normed, gathered, w_buf,
     zs, zr, ys, yr, ms, mr, ls, ks, kr, fs, fr, ws, wr, bs, w_sem, ss, sr,
 ):
     at = Place(ny, nt)
@@ -171,6 +168,11 @@
                 others.append({"pool": lax.rem(at.p + dp, 2), "tensor": lax.rem(at.t + dt, nt)})
     meet(others)
     me = at.rank(at.p, at.t)
+    step, arrive, finish = gather_blocks(
+        at, hidden, lambda rank: gathered.at[rank], (zs, zr, ys, yr, ms, mr, ls),
+        lambda rank: use(rank),
+    )
+    step(0)
 
     wide = hidden[...].astype(jnp.float32)
     squares[...] = lax.dot_general(
@@ -207,25 +209,24 @@
                 sends.append(remote(kv.at[:, head], blocks.at[me], ks.at[slot], kr.at[slot], device))
                 sends[-1].start()
 
-    total = squares[...]
-    for i, copy in enumerate(square_copies):
-        copy.wait_recv()
-        total = total + squares_all[i]
-    scale = lax.rsqrt(total * (1.0 / (width * ranks)) + 1e-05)
-    scale = jnp.transpose(jnp.concatenate([scale] * 16, axis=0))
-    for c in range(width // 128):
-        lanes = slice(c * 128, (c + 1) * 128)
-        normed[:, lanes] = (
-            hidden[:, lanes].astype(jnp.float32) * scale * gain[:, lanes]
-        ).astype(normed.dtype)
-
     def use(rank):
         load(rank).wait()
-        raw[...] += jnp.dot(gathered[rank], w_buf[rank], preferred_element_type=jnp.float32)
-
-    ring, from_across, arrive, finish = gather_blocks(
-        at, normed, lambda rank: gathered.at[rank], (zs, zr, ys, yr, ms, mr, ls), use
-    )
+        start = pl.multiple_of(rank * width, width)
+        for c in range(width // 128):
+            lanes = slice(c * 128, (c + 1) * 128)
+            features = pl.ds(pl.multiple_of(start + c * 128, 128), 128)
+            normed[:, lanes] = (
+                gathered[rank, :, lanes].astype(jnp.float32) * scales[...] * gain[:, features]
+            ).astype(normed.dtype)
+        raw[...] += jnp.dot(normed[...], w_buf[rank], preferred_element_type=jnp.float32)
+
+    def sum_squares():
+        total = squares[...]
+        for i, copy in enumerate(square_copies):
+            copy.wait_recv()
+            total = total + squares_all[i]
+        scale = lax.rsqrt(total * (1.0 / (width * ranks)) + 1e-05)
+        scales[...] = jnp.transpose(jnp.concatenate([scale] * 16, axis=0))
 
     def block_from(dz, dp):
         return at.rank(lax.rem(at.p + dp, 2), at.chip(at.down(at.z, dz), at.y))
@@ -243,18 +244,17 @@
                 sends.append(remote(src, here, fs.at[slot], fr.at[slot], at.across))
                 sends[-1].start()
 
-    ring(0)
     forward(0)
     swap.start()
-    load(me).wait()
-    raw[...] = jnp.dot(normed[...], w_buf[me], preferred_element_type=jnp.float32)
-    for s in range(1, nz):
-        ring(s)
-        from_across(s - 1)
-        forward(s)
+    gathered[me] = hidden[...]
+    raw[...] = jnp.zeros_like(raw)
+    sum_squares()
+    use(me)
+    for s in range(1, nz + 1):
+        step(s)
+        if s < nz:
+            forward(s)
         arrive(s - 1)
-    from_across(nz - 1)
-    arrive(nz - 1)
     finish()
     if ny == 2:
         for dz in range(nz):
@@ -295,6 +295,7 @@
         scratch_shapes=[
             pltpu.VMEM((8, rows), jnp.float32),
             pltpu.VMEM((ranks - 1, 8, rows), jnp.float32),
+            pltpu.VMEM((rows, 128), jnp.float32),
             pltpu.VMEM((rows, width), hidden.dtype),
             pltpu.VMEM((ranks, rows, width), hidden.dtype),
             pltpu.VMEM((ranks, width, columns), w_query.dtype),
@@ -423,14 +424,9 @@
     def block_of(rank):
         return out.at[:, pl.ds(pl.multiple_of(rank * width, width), width)]
 
-    ring, from_across, arrive, finish = gather_blocks(
-        at, final, block_of, (zs, zr, ys, yr, ms, mr, ls)
-    )
-    ring(0)
-    for s in range(1, nz):
-        ring(s)
-        from_across(s - 1)
-    from_across(nz - 1)
+    step, arrive, finish = gather_blocks(at, final, block_of, (zs, zr, ys, yr, ms, mr, ls))
+    for s in range(nz + 1):
+        step(s)
     for s in range(nz):
         arrive(s)
     finish()
@@ -499,6 +495,106 @@
     )(heads, w_out, w_mate)
 
 
+def attention_kernel(
+    table, lengths, raw, cosine, sine, draft_k, draft_v, draft_bias, blocks, out, keys, values, sems
+):
+    request = pl.program_id(0)
+    requests, context, head_dim = keys.shape
+    block_len = blocks.shape[2]
+    listed = context // block_len
+
+    def copies(r, j):
+        here = pl.ds(pl.multiple_of(j * block_len, block_len), block_len)
+        block = table[r, j]
+        return [
+            pltpu.make_async_copy(blocks.at[block, 0], keys.at[r, here, :], sems.at[0, r, j]),
+            pltpu.make_async_copy(blocks.at[block, 1], values.at[r, here, :], sems.at[1, r, j]),
+        ]
+
+    @pl.when(request == 0)
+    def _():
+        def start(i, carry):
+            for copy in copies(i // listed, lax.rem(i, listed)):
+                copy.start()
+            return carry
+
+        lax.fori_loop(0, requests * listed, start, 0)
+
+    def arrived(j, carry):
+        for copy in copies(request, j):
+            copy.wait()
+        return carry
+
+    lax.fori_loop(0, listed, arrived, 0)
+    both = (((1,), (1,)), ((), ()))
+    f32 = jnp.float32
+    valid = lax.broadcasted_iota(jnp.int32, (1, context), 1) < lengths[request]
+    for h in range(raw.shape[1] // head_dim):
+        lanes = slice(h * head_dim, (h + 1) * head_dim)
+        query = raw[:, lanes]
+        swapped = jnp.concatenate(
+            [query[:, head_dim // 2 :], query[:, : head_dim // 2]], axis=1
+        )
+        query = query * cosine[...] + swapped * sine[...]
+        query = (query * head_dim ** (-0.5)).astype(jnp.bfloat16)
+        cache = lax.dot_general(query, keys[request], both, preferred_element_type=f32)
+        cache = jnp.where(valid, cache, -jnp.inf)
+        draft = lax.dot_general(query, draft_k[...], both, preferred_element_type=f32)
+        draft = draft + draft_bias[0]
+        peak = jnp.maximum(
+            jnp.max(cache, axis=-1, keepdims=True), jnp.max(draft, axis=-1, keepdims=True)
+        )
+        cache = jnp.exp(cache - peak)
+        draft = jnp.exp(draft - peak)
+        share = 1.0 / (
+            jnp.sum(cache, axis=-1, keepdims=True) + jnp.sum(draft, axis=-1, keepdims=True)
+        )
+        cache = (cache * share).astype(jnp.bfloat16)
+        draft = (draft * share).astype(jnp.bfloat16)
+        rows = jnp.dot(cache, values[request], preferred_element_type=f32)
+        rows = rows + jnp.dot(draft, draft_v[...], preferred_element_type=f32)
+        out[:, lanes] = rows.astype(out.dtype)
+
+
+def attention(raw, cosine, sine, draft_k, draft_v, draft_bias, blocks, table, lengths):
+    rows, columns = raw.shape
+    requests, listed = table.shape
+    drafts = rows // requests
+    block_len, head_dim = blocks.shape[2:]
+    context = listed * block_len
+
+    def by_rows(width):
+        return pl.BlockSpec((drafts, width), lambda r, *_: (r, 0))
+
+    return pl.pallas_call(
+        attention_kernel,
+        out_shape=jax.ShapeDtypeStruct((rows, columns), jnp.bfloat16),
+        grid_spec=pltpu.PrefetchScalarGridSpec(
+            num_scalar_prefetch=2,
+            grid=(requests,),
+            in_specs=[
+                by_rows(columns),
+                by_rows(head_dim),
+                by_rows(head_dim),
+                by_rows(head_dim),
+                by_rows(head_dim),
+                pl.BlockSpec((1, drafts, drafts), lambda r, *_: (r, 0, 0)),
+                pl.BlockSpec(memory_space=pl.ANY),
+            ],
+            out_specs=by_rows(columns),
+            scratch_shapes=[
+                pltpu.VMEM((requests, context, head_dim), blocks.dtype),
+                pltpu.VMEM((requests, context, head_dim), blocks.dtype),
+                pltpu.SemaphoreType.DMA((2, requests, listed)),
+            ],
+        ),
+        compiler_params=pltpu.CompilerParams(
+            dimension_semantics=("arbitrary",), vmem_limit_bytes=VMEM_LIMIT
+        ),
+        name="mid",
+    )(table, lengths, raw, cosine, sine, draft_k, draft_v, draft_bias, blocks)
+
+
 def shards(
     hidden, norm_gain, w_query, w_out, kv_pool, draft_kv, block_table, cached_len, draft_pos
 ):
@@ -509,60 +605,30 @@
     kv_heads = kv_pool.shape[1]
     block_len = kv_pool.shape[3]
     head_dim = kv_pool.shape[4]
-    requests = draft_pos.shape[0]
     drafts = draft_pos.shape[1]
-    listed = block_table.shape[1]
-    context = listed * block_len
-    local_heads = w_query.shape[1] // head_dim
     group_size = devices // kv_heads
     own_head = my_rank // group_size
-    width = hidden.shape[1]
-    gain = lax.dynamic_slice_in_dim(norm_gain, my_rank * width, width).reshape(1, width)
+    gain = norm_gain.reshape(1, -1)
     raw_queries, arrived, w_mate = front(
         ny, nt, group_size, hidden, gain, kv_pool, w_out, w_query
     )
     positions = (cached_len[:, None] + draft_pos).reshape(-1)
-    query_heads = (
-        rotate(raw_queries.reshape(-1, local_heads, head_dim), positions) * head_dim ** (-0.5)
-    ).astype(jnp.bfloat16)
-    query_heads = query_heads.reshape(requests, drafts, local_heads, head_dim)
+    half_dim = head_dim // 2
+    frequency = 500000.0 ** (-(jnp.arange(half_dim, dtype=jnp.float32) * 2.0) / head_dim)
+    angles = positions.astype(jnp.float32)[:, None] * frequency[None, :]
+    cosine, sine = jnp.cos(angles), jnp.sin(angles)
+    cosine = jnp.concatenate([cosine, cosine], axis=-1)
+    sine = jnp.concatenate([-sine, sine], axis=-1)
     own_draft = lax.dynamic_slice_in_dim(draft_kv, own_head * head_dim, head_dim, axis=2)
-    own_draft = own_draft.reshape(requests, drafts, 2, head_dim)
-    draft_keys = own_draft[:, :, 0]
-    draft_values = own_draft[:, :, 1]
     draft_valid = (draft_pos[:, None, :] < draft_pos[:, :, None]) | jnp.eye(drafts, dtype=bool)[
         None
     ]
-    arrived = arrived.reshape(-1, 2, block_len, head_dim)
-    gathered_blocks = arrived[block_table]
-    cache_keys = gathered_blocks[:, :, 0].reshape(requests, context, head_dim)
-    cache_values = gathered_blocks[:, :, 1].reshape(requests, context, head_dim)
-    cache_scores = jnp.einsum(
-        "rqhd,rkd->rqhk", query_heads, cache_keys, preferred_element_type=jnp.float32
-    )
-    cache_valid = jnp.arange(context)[None, :] < cached_len[:, None]
-    cache_scores = jnp.where(cache_valid[:, None, None, :], cache_scores, -jnp.inf)
-    draft_scores = jnp.einsum(
-        "rqhd,rpd->rqhp", query_heads, draft_keys, preferred_element_type=jnp.float32
-    )
-    draft_scores = jnp.where(draft_valid[:, :, None, :], draft_scores, -jnp.inf)
-    row_peak = jnp.maximum(
-        jnp.max(cache_scores, axis=-1, keepdims=True), jnp.max(draft_scores, axis=-1, keepdims=True)
-    )
-    cache_weights = jnp.exp(cache_scores - row_peak)
-    draft_weights = jnp.exp(draft_scores - row_peak)
-    weight_sum = jnp.sum(cache_weights, axis=-1, keepdims=True) + jnp.sum(
-        draft_weights, axis=-1, keepdims=True
-    )
-    cache_probs = (cache_weights / weight_sum).astype(jnp.bfloat16)
-    draft_probs = (draft_weights / weight_sum).astype(jnp.bfloat16)
-    head_rows = jnp.einsum(
-        "rqhk,rkd->rqhd", cache_probs, cache_values, preferred_element_type=jnp.float32
-    )
-    head_rows = head_rows + jnp.einsum(
-        "rqhp,rpd->rqhd", draft_probs, draft_values, preferred_element_type=jnp.float32
-    )
-    heads_out = head_rows.astype(jnp.bfloat16).reshape(requests * drafts, local_heads * head_dim)
+    draft_bias = jnp.where(draft_valid, 0.0, -jnp.inf).astype(jnp.float32)
+    blocks = arrived.reshape(-1, 2, block_len, head_dim)
+    heads_out = attention(
+        raw_queries, cosine, sine, own_draft[:, 0], own_draft[:, 1], draft_bias,
+        blocks, block_table, cached_len,
+    )
     return back(ny, nt, heads_out, w_out, w_mate)
 
 

time: 209 us -> 187 us (0.89)
  local copies, waits for them, and re-layouts: 21.9 us -> 8.45 us
  matrix products: 6.44 us -> 0 us
  other arithmetic: 7.91 us -> 4.06 us
    pallas_call x0 -> x1, Pallas kernels: none -> 12.5 us  [attention(): pl.pallas_call(attention_kernel, out_shape=jax.ShapeDtypeStruct((rows, co...]
    pallas_call x1, Pallas kernels: 83.3 us -> 75.9 us  [front(): pl.pallas_call(functools.partial(front_kernel, ny, nt, group_size), out_s...]
    dot_general x4 -> x0, matrix products: 6.44 us -> none  [the longest x1 3.69 us: shards(): jnp.einsum('rqhd,rkd->rqhk', query_heads, cache_keys, preferred_element_t...]
    concatenate x4 -> x0, local copies, waits for them, and re-layouts: 5.01 us -> none  [rotate(): jnp.concatenate([first_half * cosine - second_half * sine_part, second_ha...]
    reduce_sum x2 -> x0, other arithmetic: 4.56 us -> none  [the longest x1 4.4 us: shards(): jnp.sum(cache_weights, axis=-1, keepdims=True)]
    gather x1 -> x0, local copies, waits for them, and re-layouts: 3.72 us -> none  [shards(): gathered_blocks = arrived[block_table]]
    pallas_call x1, Pallas kernels: 88.5 us -> 85.1 us  [back(): pl.pallas_call(functools.partial(back_kernel, ny, nt), out_shape=jax.Shap...]
    unnamed x14 -> x1, local copies, waits for them, and re-layouts: 7.03 us -> 6.2 us
where the time goes in v3:
time: 187 us; the launch traced here: 186 us
  Pallas kernels  174 us (93%)
  local copies, waits for them, and re-layouts  8.45 us (5%)
  other arithmetic  4.06 us (2%)
    pallas_call x1, Pallas kernels, back(): pl.pallas_call(functools.partial(back_kernel, ny, nt), out_shape=jax.Shap...  85.1 us
    pallas_call x1, Pallas kernels, front(): pl.pallas_call(functools.partial(front_kernel, ny, nt, group_size), out_s...  75.9 us
    pallas_call x1, Pallas kernels, attention(): pl.pallas_call(attention_kernel, out_shape=jax.ShapeDtypeStruct((rows, co...  12.5 us
    unnamed x1, local copies, waits for them, and re-layouts  6.2 us

profile of v3, /device:TPU:0, one launch (start us, length us, event | category | flops | bytes accessed | tf_op | source)
XLA Modules:
  0.0 186.1 jit_solution(10871433879214468006)
XLA Ops:
  0.0 0.8 add_convert_fusion
  0.8 0.1 convert_element_type.11
  0.9 1.6 or_select_fusion.draft_bias
  2.4 1.5 constant_dynamic-slice_fusion.1
  3.9 0.7 copy_bitcast_fusion
  4.6 0.8 fusion
  5.4 0.9 pad_maximum_fusion
  6.3 75.9 %front.1 = (f32[384,512]{1,0:T(8,128)}, bf16[16,2,2,128,128]{4,3,2,1,0:T(8,128)(2,1)}, bf16[512,4096]{1,0:T(8,128)(2,1)}) custom-call(bf16[384,512]{1,0:T(8,128)(2,1)} %hidden.1, f32[1,8192]{1,0:T(1,128)} %bitcast.7, bf16[2,8,2,128,128]{4,3,2,1,0:T(8,128)(2,1)} %kv.1, bf16[512,8192]{1,0:T(8,128)(2,1)} %w_own.1, bf16[8192,512]{1,0:T(8,128)(2,1)} %w_query.1), custom_call_target="tpu_custom_call" | custom-call | tf_op jit(solution)/shard_map/front/pallas_call | solution.py:281
  82.3 12.5 %mid.1.heads = bf16[384,512]{1,0:T(8,128)(2,1)} custom-call(s32[4,8]{1,0:T(4,128)} %table.1, s32[4]{0:T(128)} %lengths.1, f32[384,512]{1,0:T(8,128)} %get-tuple-element.8.raw, f32[384,128]{1,0:T(8,128)} %get-tuple-element.16.cosine, f32[384,128]{1,0:T(8,128)} %get-tuple-element.17.sine, bf16[384,128]{1,0:T(8,128)(2,1)} %get-tuple-element.19.draft_k, ...), custom_call_target="tpu_custom_call" | custom-call | tf_op jit(solution)/shard_map/mid/pallas_call | solution.py:569
  94.8 85.1 %back.1 = bf16[384,8192]{1,0:T(8,128)(2,1)} custom-call(bf16[384,512]{1,0:T(8,128)(2,1)} %mid.1.heads, bf16[512,8192]{1,0:T(8,128)(2,1)} %w_own.1, bf16[512,4096]{1,0:T(8,128)(2,1)} %get-tuple-element.10.w_mate), custom_call_target="tpu_custom_call" | custom-call | tf_op jit(solution)/shard_map/back/pallas_call | solution.py:457
  179.9 6.2 %copy.17 = bf16[384,8192]{1,0:T(8,128)(2,1)} copy(bf16[384,8192]{1,0:T(8,128)(2,1)} %back.1) | data formatting | bytes 12582912
  (2 shorter events, 0.0 us)

commit v4 on v3

--- a/solution.py
+++ b/solution.py
@@ -2,6 +2,7 @@
 
 import jax
 import jax.numpy as jnp
+import numpy as np
 from jax import lax
 from jax.experimental import pallas as pl
 from jax.experimental.pallas import tpu as pltpu
@@ -66,7 +67,7 @@
     pl.semaphore_wait(barrier, len(devices))
 
 
-def gather_blocks(at, own, block_of, sems, use=None):
+def gather_blocks(at, own, block_of, sems, use=None, keep_last=False):
     zs, zr, ys, yr, ms, mr, ls = sems
     nz, ny = at.nz, at.ny
     part = own.shape[0] // PIECES
@@ -77,10 +78,8 @@
     def block(p, z, y, h):
         return rows(block_of(at.rank(p, at.chip(z, y))), h)
 
-    keep = None
-    if use is None:
+    if keep_last:
         keep = pltpu.make_async_copy(own, block_of(at.rank(at.p, at.t)), ls)
-        keep.start()
     started = []
 
     def send(src, dst, send_sem, recv_sem, device):
@@ -105,12 +104,14 @@
             remote(there, there, ys.at[s, h], yr.at[s, h], at.across).wait_recv()
             send(there, there, ms.at[nz + s, h], mr.at[nz + s, h], at.mate)
 
-    def step(s):
-        for h in range(PIECES):
+    def step(s, pieces=range(PIECES)):
+        for h in pieces:
             if s < nz:
                 ring(s, h)
             if s > 0:
                 from_across(s - 1, h)
+            if keep_last and s == 0 and h == PIECES - 1:
+                keep.start()
 
     def arrive(s):
         z = at.down(at.z, s)
@@ -128,7 +129,7 @@
     def finish():
         for copy in started:
             copy.wait_send()
-        if keep is not None:
+        if keep_last:
             keep.wait()
 
     return step, arrive, finish
@@ -197,7 +198,8 @@
         w_mate, ws, wr, at.mate,
     )
     sends = []
-    for dz in range(nz):
+
+    def send_blocks(dz):
         for dp in range(2):
             if dz + dp > 0:
                 device = {
@@ -208,6 +210,8 @@
                 head = head_of(device["pool"], device["tensor"])
                 sends.append(remote(kv.at[:, head], blocks.at[me], ks.at[slot], kr.at[slot], device))
                 sends[-1].start()
+
+    send_blocks(0)
 
     def use(rank):
         load(rank).wait()
@@ -253,7 +257,9 @@
     for s in range(1, nz + 1):
         step(s)
         if s < nz:
-            forward(s)
+            send_blocks(s)
+        if s > 1:
+            forward(s - 1)
         arrive(s - 1)
     finish()
     if ny == 2:
@@ -339,8 +345,7 @@
             src = w_mate.at[:, pl.ds(pl.multiple_of(t * width, width), width)]
         return pltpu.make_async_copy(src, w_buf.at[which, t], w_sem.at[which, t])
 
-    def chunk(s):
-        return at.down(at.z, s + 1)
+    part = heads.shape[0] // PIECES
 
     def chip_of(s, y):
         return at.chip(lax.rem(at.z + 2 * nz - 1 - s, nz), y)
@@ -363,88 +368,112 @@
     trade.start()
     trade.wait()
 
-    def term(t):
-        load(0, t).wait()
-        load(1, t).wait()
-        return jnp.dot(heads[...], w_buf[0, t], preferred_element_type=jnp.float32) + jnp.dot(
-            heads_mate[...], w_buf[1, t], preferred_element_type=jnp.float32
-        )
-
-    def across_copies(s):
+    def rows_of(i):
+        return pl.ds(pl.multiple_of(lax.rem(i, PIECES) * part, part), part)
+
+    def wait_loads(y):
+        def body(s, carry):
+            t = chip_of(s, y)
+            load(0, t).wait()
+            load(1, t).wait()
+            return carry
+
+        lax.fori_loop(0, nz, body, 0)
+
+    def term(i, y):
+        t = chip_of(i // PIECES, y)
+        return jnp.dot(
+            heads[rows_of(i), :], w_buf[0, t], preferred_element_type=jnp.float32
+        ) + jnp.dot(heads_mate[rows_of(i), :], w_buf[1, t], preferred_element_type=jnp.float32)
+
+    def across_copies(i):
         return [
-            remote(y_send.at[s], y_recv.at[s], ps.at[s], pr.at[s], at.across),
-            remote(y_send_scale.at[s], y_recv_scale.at[s], pss.at[s], psr.at[s], at.across),
+            remote(y_send.at[i], y_recv.at[i], ps.at[i], pr.at[i], at.across),
+            remote(y_send_scale.at[i], y_recv_scale.at[i], pss.at[i], psr.at[i], at.across),
         ]
 
-    def ring_copies(s):
+    def ring_copies(i):
         return [
-            remote(z_send.at[s], z_recv.at[s], qs.at[s], qr.at[s], at.next),
-            remote(z_send_scale.at[s], z_recv_scale.at[s], qss.at[s], qsr.at[s], at.next),
+            remote(z_send.at[i], z_recv.at[i], qs.at[i], qr.at[i], at.next),
+            remote(z_send_scale.at[i], z_recv_scale.at[i], qss.at[i], qsr.at[i], at.next),
         ]
 
     if ny == 2:
-
-        def send_across(s, carry):
-            code(term(chip_of(s, 1 - at.y)), y_send.at[s], y_send_scale.at[s])
-            for copy in across_copies(s):
+        wait_loads(1 - at.y)
+
+        def send_across(i, carry):
+            code(term(i, 1 - at.y), y_send.at[i], y_send_scale.at[i])
+            for copy in across_copies(i):
                 copy.start()
             return carry
 
-        lax.fori_loop(0, nz, send_across, 0)
-
-    def total(s):
-        value = term(chip_of(s, at.y))
+        lax.fori_loop(0, nz * PIECES, send_across, 0)
+    wait_loads(at.y)
+
+    def total(i):
+        value = term(i, at.y)
         if ny == 2:
-            for copy in across_copies(s):
+            for copy in across_copies(i):
                 copy.wait_recv()
-            value = value + decode(y_recv.at[s], y_recv_scale.at[s])
+            value = value + decode(y_recv.at[i], y_recv_scale.at[i])
         return value
 
-    def ring_received(s):
-        for copy in ring_copies(s):
+    def ring_received(i):
+        for copy in ring_copies(i):
             copy.wait_recv()
-        return decode(z_recv.at[s], z_recv_scale.at[s])
-
-    def ring_send(s, value):
-        code(value, z_send.at[s], z_send_scale.at[s])
-        for copy in ring_copies(s):
+        return decode(z_recv.at[i], z_recv_scale.at[i])
+
+    def ring_send(i, value):
+        code(value, z_send.at[i], z_send_scale.at[i])
+        for copy in ring_copies(i):
             copy.start()
 
-    ring_send(0, total(0))
-
-    def ring_step(s, carry):
-        value = total(s)
-        ring_send(s, value + ring_received(s - 1))
+    def ring_first(i, carry):
+        ring_send(i, total(i))
         return carry
 
-    lax.fori_loop(1, nz - 1, ring_step, 0)
-    value = total(nz - 1)
-    final[...] = (value + ring_received(nz - 2)).astype(final.dtype)
+    lax.fori_loop(0, PIECES, ring_first, 0)
+
+    def ring_step(i, carry):
+        value = total(i)
+        ring_send(i, value + ring_received(i - PIECES))
+        return carry
+
+    lax.fori_loop(PIECES, (nz - 1) * PIECES, ring_step, 0)
 
     def block_of(rank):
         return out.at[:, pl.ds(pl.multiple_of(rank * width, width), width)]
 
-    step, arrive, finish = gather_blocks(at, final, block_of, (zs, zr, ys, yr, ms, mr, ls))
-    for s in range(nz + 1):
+    step, arrive, finish = gather_blocks(
+        at, final, block_of, (zs, zr, ys, yr, ms, mr, ls), keep_last=True
+    )
+    for h in range(PIECES):
+        i = (nz - 1) * PIECES + h
+        value = total(i)
+        final[h * part : (h + 1) * part, :] = (value + ring_received(i - PIECES)).astype(
+            final.dtype
+        )
+        step(0, (h,))
+    for s in range(1, nz + 1):
         step(s)
     for s in range(nz):
         arrive(s)
     finish()
 
-    def sent(s, carry):
+    def sent(i, carry):
         if ny == 2:
-            for copy in across_copies(s):
+            for copy in across_copies(i):
                 copy.wait_send()
         return carry
 
-    lax.fori_loop(0, nz, sent, 0)
+    lax.fori_loop(0, nz * PIECES, sent, 0)
 
     def ring_sent(s, carry):
         for copy in ring_copies(s):
             copy.wait_send()
         return carry
 
-    lax.fori_loop(0, nz - 1, ring_sent, 0)
+    lax.fori_loop(0, (nz - 1) * PIECES, ring_sent, 0)
 
 
 def back(ny, nt, heads, w_out, w_mate):
@@ -466,26 +495,26 @@
         scratch_shapes=[
             pltpu.VMEM((rows, depth), heads.dtype),
             pltpu.VMEM((2, nt, depth, width), w_out.dtype),
-            pltpu.VMEM((nz, rows, width), jnp.int16),
-            pltpu.VMEM((nz, rows, width), jnp.int16),
-            pltpu.VMEM((nz - 1, rows, width), jnp.int16),
-            pltpu.VMEM((nz - 1, rows, width), jnp.int16),
-            pltpu.VMEM((nz, 8, width), f32),
-            pltpu.VMEM((nz, 8, width), f32),
-            pltpu.VMEM((nz - 1, 8, width), f32),
-            pltpu.VMEM((nz - 1, 8, width), f32),
+            pltpu.VMEM((nz * PIECES, rows // PIECES, width), jnp.int16),
+            pltpu.VMEM((nz * PIECES, rows // PIECES, width), jnp.int16),
+            pltpu.VMEM(((nz - 1) * PIECES, rows // PIECES, width), jnp.int16),
+            pltpu.VMEM(((nz - 1) * PIECES, rows // PIECES, width), jnp.int16),
+            pltpu.VMEM((nz * PIECES, 8, width), f32),
+            pltpu.VMEM((nz * PIECES, 8, width), f32),
+            pltpu.VMEM(((nz - 1) * PIECES, 8, width), f32),
+            pltpu.VMEM(((nz - 1) * PIECES, 8, width), f32),
             pltpu.VMEM((rows, width), jnp.bfloat16),
             dma,
             dma,
             dma((2, nt)),
-            dma((nz,)),
-            dma((nz,)),
-            dma((nz,)),
-            dma((nz,)),
-            dma((nz,)),
-            dma((nz,)),
-            dma((nz,)),
-            dma((nz,)),
+            dma((nz * PIECES,)),
+            dma((nz * PIECES,)),
+            dma((nz * PIECES,)),
+            dma((nz * PIECES,)),
+            dma((nz * PIECES,)),
+            dma((nz * PIECES,)),
+            dma((nz * PIECES,)),
+            dma((nz * PIECES,)),
         ]
         + gather_sems(ny, nz),
         compiler_params=pltpu.CompilerParams(
@@ -496,7 +525,7 @@
 
 
 def attention_kernel(
-    table, lengths, raw, cosine, sine, draft_k, draft_v, draft_bias, blocks, out, keys, values, sems
+    table, lengths, head, raw, depth_down, depth_along, frequency, draft_kv, blocks, out, keys, values, sems
 ):
     request = pl.program_id(0)
     requests, context, head_dim = keys.shape
@@ -529,18 +558,31 @@
     both = (((1,), (1,)), ((), ()))
     f32 = jnp.float32
     valid = lax.broadcasted_iota(jnp.int32, (1, context), 1) < lengths[request]
+    drafts = raw.shape[0]
+    angles = (lengths[request] + depth_down[...]).astype(f32) * frequency[...]
+    cosine = jnp.cos(angles)
+    sine = jnp.sin(angles)
+    sine = jnp.where(
+        lax.broadcasted_iota(jnp.int32, (1, head_dim), 1) < head_dim // 2, -sine, sine
+    )
+    square = (drafts, drafts)
+    draft_valid = (depth_along[0] < depth_down[...]) | (
+        lax.broadcasted_iota(jnp.int32, square, 0) == lax.broadcasted_iota(jnp.int32, square, 1)
+    )
+    draft_k = draft_kv[:, 0, :]
+    draft_v = draft_kv[:, 1, :]
     for h in range(raw.shape[1] // head_dim):
         lanes = slice(h * head_dim, (h + 1) * head_dim)
         query = raw[:, lanes]
         swapped = jnp.concatenate(
             [query[:, head_dim // 2 :], query[:, : head_dim // 2]], axis=1
         )
-        query = query * cosine[...] + swapped * sine[...]
+        query = query * cosine + swapped * sine
         query = (query * head_dim ** (-0.5)).astype(jnp.bfloat16)
         cache = lax.dot_general(query, keys[request], both, preferred_element_type=f32)
         cache = jnp.where(valid, cache, -jnp.inf)
-        draft = lax.dot_general(query, draft_k[...], both, preferred_element_type=f32)
-        draft = draft + draft_bias[0]
+        draft = lax.dot_general(query, draft_k, both, preferred_element_type=f32)
+        draft = jnp.where(draft_valid, draft, -jnp.inf)
         peak = jnp.maximum(
             jnp.max(cache, axis=-1, keepdims=True), jnp.max(draft, axis=-1, keepdims=True)
         )
@@ -552,11 +594,11 @@
         cache = (cache * share).astype(jnp.bfloat16)
         draft = (draft * share).astype(jnp.bfloat16)
         rows = jnp.dot(cache, values[request], preferred_element_type=f32)
-        rows = rows + jnp.dot(draft, draft_v[...], preferred_element_type=f32)
+        rows = rows + jnp.dot(draft, draft_v, preferred_element_type=f32)
         out[:, lanes] = rows.astype(out.dtype)
 
 
-def attention(raw, cosine, sine, draft_k, draft_v, draft_bias, blocks, table, lengths):
+def attention(raw, depth, frequency, draft_kv, blocks, table, lengths, head):
     rows, columns = raw.shape
     requests, listed = table.shape
     drafts = rows // requests
@@ -570,15 +612,14 @@
         attention_kernel,
         out_shape=jax.ShapeDtypeStruct((rows, columns), jnp.bfloat16),
         grid_spec=pltpu.PrefetchScalarGridSpec(
-            num_scalar_prefetch=2,
+            num_scalar_prefetch=3,
             grid=(requests,),
             in_specs=[
                 by_rows(columns),
-                by_rows(head_dim),
-                by_rows(head_dim),
-                by_rows(head_dim),
-                by_rows(head_dim),
-                pl.BlockSpec((1, drafts, drafts), lambda r, *_: (r, 0, 0)),
+                by_rows(1),
+                pl.BlockSpec((1, 1, drafts), lambda r, *_: (r, 0, 0)),
+                pl.BlockSpec((1, head_dim), lambda r, *_: (0, 0)),
+                pl.BlockSpec((drafts, 2, head_dim), lambda r, table, lengths, head: (r, 0, head[0])),
                 pl.BlockSpec(memory_space=pl.ANY),
             ],
             out_specs=by_rows(columns),
@@ -592,7 +633,10 @@
             dimension_semantics=("arbitrary",), vmem_limit_bytes=VMEM_LIMIT
         ),
         name="mid",
-    )(table, lengths, raw, cosine, sine, draft_k, draft_v, draft_bias, blocks)
+    )(
+        table, lengths, head, raw, depth.reshape(rows, 1), depth[:, None, :], frequency,
+        draft_kv, blocks,
+    )
 
 
 def shards(
@@ -605,29 +649,18 @@
     kv_heads = kv_pool.shape[1]
     block_len = kv_pool.shape[3]
     head_dim = kv_pool.shape[4]
-    drafts = draft_pos.shape[1]
     group_size = devices // kv_heads
     own_head = my_rank // group_size
     gain = norm_gain.reshape(1, -1)
     raw_queries, arrived, w_mate = front(
         ny, nt, group_size, hidden, gain, kv_pool, w_out, w_query
     )
-    positions = (cached_len[:, None] + draft_pos).reshape(-1)
-    half_dim = head_dim // 2
-    frequency = 500000.0 ** (-(jnp.arange(half_dim, dtype=jnp.float32) * 2.0) / head_dim)
-    angles = positions.astype(jnp.float32)[:, None] * frequency[None, :]
-    cosine, sine = jnp.cos(angles), jnp.sin(angles)
-    cosine = jnp.concatenate([cosine, cosine], axis=-1)
-    sine = jnp.concatenate([-sine, sine], axis=-1)
-    own_draft = lax.dynamic_slice_in_dim(draft_kv, own_head * head_dim, head_dim, axis=2)
-    draft_valid = (draft_pos[:, None, :] < draft_pos[:, :, None]) | jnp.eye(drafts, dtype=bool)[
-        None
-    ]
-    draft_bias = jnp.where(draft_valid, 0.0, -jnp.inf).astype(jnp.float32)
+    half = np.arange(head_dim // 2, dtype=np.float64)
+    frequency = np.tile(500000.0 ** (-2.0 * half / head_dim), 2).astype(np.float32)
     blocks = arrived.reshape(-1, 2, block_len, head_dim)
     heads_out = attention(
-        raw_queries, cosine, sine, own_draft[:, 0], own_draft[:, 1], draft_bias,
-        blocks, block_table, cached_len,
+        raw_queries, draft_pos, jnp.asarray(frequency)[None, :], draft_kv, blocks,
+        block_table, cached_len, jnp.reshape(own_head, (1,)),
     )
     return back(ny, nt, heads_out, w_out, w_mate)
 

time: 187 us -> 177 us (0.947)
  Pallas kernels: 174 us -> 169 us
  other arithmetic: 4.06 us -> 0 us
    pallas_call x1, Pallas kernels: 75.9 us -> 72.2 us  [front(): pl.pallas_call(functools.partial(front_kernel, ny, nt, group_size), out_s...]
where the time goes in v4:
time: 177 us
  Pallas kernels  169 us (95%)
  local copies, waits for them, and re-layouts  7.72 us (4%)
    pallas_call x1, Pallas kernels, back(): pl.pallas_call(functools.partial(back_kernel, ny, nt), out_shape=jax.Shap...  83.6 us
    pallas_call x1, Pallas kernels, front(): pl.pallas_call(functools.partial(front_kernel, ny, nt, group_size), out_s...  72.2 us
    pallas_call x1, Pallas kernels, attention(): pl.pallas_call(attention_kernel, out_shape=jax.ShapeDtypeStruct((rows, co...  13.2 us
    unnamed x1, local copies, waits for them, and re-layouts  6.2 us

profile of v4, /device:TPU:0, one launch (start us, length us, event | category | flops | bytes accessed | tf_op | source)
XLA Modules:
  0.0 176.8 jit_solution(13207771383794598653)
XLA Ops:
  0.0 1.5 reshape.16.depth_down
  1.5 72.2 %front.1 = (f32[384,512]{1,0:T(8,128)}, bf16[16,2,2,128,128]{4,3,2,1,0:T(8,128)(2,1)}, bf16[512,4096]{1,0:T(8,128)(2,1)}) custom-call(bf16[384,512]{1,0:T(8,128)(2,1)} %hidden.1, f32[1,8192]{1,0:T(1,128)} %bitcast.5, bf16[2,8,2,128,128]{4,3,2,1,0:T(8,128)(2,1)} %kv.1, bf16[512,8192]{1,0:T(8,128)(2,1)} %w_own.1, bf16[8192,512]{1,0:T(8,128)(2,1)} %w_query.1), custom_call_target="tpu_custom_call" | custom-call | tf_op jit(solution)/shard_map/front/pallas_call | solution.py:287
  73.7 13.2 %mid.1.heads = bf16[384,512]{1,0:T(8,128)(2,1)} custom-call(s32[4,8]{1,0:T(4,128)} %table.1, s32[4]{0:T(128)} %lengths.1, s32[1]{0:T(128)} %bitcast.head, f32[384,512]{1,0:T(8,128)} %get-tuple-element.8.raw, s32[384,1]{1,0:T(8,128)} %reshape.16.depth_down, s32[4,1,96]{2,1,0:T(1,128)} %bitcast.6, f32[1,128]{1,0:T(1,128)} %constant.29.frequency, ...), custom_call_target="tpu_custom_call" | custom-call | tf_op jit(solution)/shard_map/mid/pallas_call | solution.py:611
  86.9 83.6 %back.1 = bf16[384,8192]{1,0:T(8,128)(2,1)} custom-call(bf16[384,512]{1,0:T(8,128)(2,1)} %mid.1.heads, bf16[512,8192]{1,0:T(8,128)(2,1)} %w_own.1, bf16[512,4096]{1,0:T(8,128)(2,1)} %get-tuple-element.10.w_mate), custom_call_target="tpu_custom_call" | custom-call | tf_op jit(solution)/shard_map/back/pallas_call | solution.py:486
  170.6 6.2 %copy.13 = bf16[384,8192]{1,0:T(8,128)(2,1)} copy(bf16[384,8192]{1,0:T(8,128)(2,1)} %back.1) | data formatting | bytes 12582912

commit v5 on v4

--- a/solution.py
+++ b/solution.py
@@ -8,7 +8,8 @@
 from jax.experimental.pallas import tpu as pltpu
 from jax.sharding import PartitionSpec as P
 
-VMEM_LIMIT = 56 * 1024 * 1024
+VMEM_LIMIT = 24 * 1024 * 1024
+FRONT_VMEM_LIMIT = 56 * 1024 * 1024
 PIECES = 2
 
 
@@ -310,7 +311,7 @@
         + [dma((2 * nz,)), dma((2 * nz,)), dma((2 * nz,)), dma((2 * nz,)), dma, dma, dma]
         + [dma((ranks,)), dma((ranks - 1,)), dma((ranks - 1,))],
         compiler_params=pltpu.CompilerParams(
-            collective_id=0, has_side_effects=True, vmem_limit_bytes=VMEM_LIMIT
+            collective_id=0, has_side_effects=True, vmem_limit_bytes=FRONT_VMEM_LIMIT
         ),
         name="front",
     )(hidden, gain, kv_pool, w_out, w_query)
@@ -571,31 +572,42 @@
     )
     draft_k = draft_kv[:, 0, :]
     draft_v = draft_kv[:, 1, :]
-    for h in range(raw.shape[1] // head_dim):
-        lanes = slice(h * head_dim, (h + 1) * head_dim)
-        query = raw[:, lanes]
+    heads = raw.shape[1] // head_dim
+    queries = []
+    for h in range(heads):
+        query = raw[:, h * head_dim : (h + 1) * head_dim]
         swapped = jnp.concatenate(
             [query[:, head_dim // 2 :], query[:, : head_dim // 2]], axis=1
         )
         query = query * cosine + swapped * sine
-        query = (query * head_dim ** (-0.5)).astype(jnp.bfloat16)
-        cache = lax.dot_general(query, keys[request], both, preferred_element_type=f32)
-        cache = jnp.where(valid, cache, -jnp.inf)
-        draft = lax.dot_general(query, draft_k, both, preferred_element_type=f32)
-        draft = jnp.where(draft_valid, draft, -jnp.inf)
-        peak = jnp.maximum(
-            jnp.max(cache, axis=-1, keepdims=True), jnp.max(draft, axis=-1, keepdims=True)
-        )
-        cache = jnp.exp(cache - peak)
-        draft = jnp.exp(draft - peak)
-        share = 1.0 / (
-            jnp.sum(cache, axis=-1, keepdims=True) + jnp.sum(draft, axis=-1, keepdims=True)
-        )
-        cache = (cache * share).astype(jnp.bfloat16)
-        draft = (draft * share).astype(jnp.bfloat16)
-        rows = jnp.dot(cache, values[request], preferred_element_type=f32)
-        rows = rows + jnp.dot(draft, draft_v, preferred_element_type=f32)
-        out[:, lanes] = rows.astype(out.dtype)
+        queries.append((query * head_dim ** (-0.5)).astype(jnp.bfloat16))
+    query = jnp.concatenate(queries, axis=0)
+    cache = lax.dot_general(query, keys[request], both, preferred_element_type=f32)
+    cache = jnp.where(valid, cache, -jnp.inf)
+    draft = lax.dot_general(query, draft_k, both, preferred_element_type=f32)
+    draft = jnp.concatenate(
+        [
+            jnp.where(draft_valid, draft[h * drafts : (h + 1) * drafts, :], -jnp.inf)
+            for h in range(heads)
+        ],
+        axis=0,
+    )
+    peak = jnp.maximum(
+        jnp.max(cache, axis=-1, keepdims=True), jnp.max(draft, axis=-1, keepdims=True)
+    )
+    cache = jnp.exp(cache - peak)
+    draft = jnp.exp(draft - peak)
+    share = 1.0 / (
+        jnp.sum(cache, axis=-1, keepdims=True) + jnp.sum(draft, axis=-1, keepdims=True)
+    )
+    cache = (cache * share).astype(jnp.bfloat16)
+    draft = (draft * share).astype(jnp.bfloat16)
+    rows = jnp.dot(cache, values[request], preferred_element_type=f32)
+    rows = rows + jnp.dot(draft, draft_v, preferred_element_type=f32)
+    for h in range(heads):
+        out[:, h * head_dim : (h + 1) * head_dim] = rows[
+            h * drafts : (h + 1) * drafts, :
+        ].astype(out.dtype)
 
 
 def attention(raw, depth, frequency, draft_kv, blocks, table, lengths, head):

time: 177 us -> 177 us (level)
  local copies, waits for them, and re-layouts: 7.72 us -> 9.93 us
  Pallas kernels: 169 us -> 167 us
    unnamed x1 -> x19, local copies, waits for them, and re-layouts: 6.2 us -> 9.08 us
    pallas_call x1, Pallas kernels: 13.2 us -> 11.2 us  [attention(): pl.pallas_call(attention_kernel, out_shape=jax.ShapeDtypeStruct((rows, co...]
where the time goes in v5:
time: 177 us
  Pallas kernels  167 us (94%)
  local copies, waits for them, and re-layouts  9.93 us (6%)
    pallas_call x1, Pallas kernels, back(): pl.pallas_call(functools.partial(back_kernel, ny, nt), out_shape=jax.Shap...  83.5 us
    pallas_call x1, Pallas kernels, front(): pl.pallas_call(functools.partial(front_kernel, ny, nt, group_size), out_s...  72.3 us
    pallas_call x1, Pallas kernels, attention(): pl.pallas_call(attention_kernel, out_shape=jax.ShapeDtypeStruct((rows, co...  11.2 us
    unnamed x19, local copies, waits for them, and re-layouts  9.08 us

profile of v5, /device:TPU:0, one launch (start us, length us, event | category | flops | bytes accessed | tf_op | source)
XLA Modules:
  0.0 177.0 jit_solution(1356746243607254057)
XLA Ops:
  0.0 0.8 reshape.16.depth_down
  0.9 0.0 copy-start.3
  0.9 0.0 copy-start.5
  0.9 0.0 copy-start.6
  0.9 0.0 copy-start.7
  0.9 0.0 copy-start.8
  0.9 72.3 %front.1 = (f32[384,512]{1,0:T(8,128)}, bf16[16,2,2,128,128]{4,3,2,1,0:T(8,128)(2,1)}, bf16[512,4096]{1,0:T(8,128)(2,1)}) custom-call(bf16[384,512]{1,0:T(8,128)(2,1)} %hidden.1, f32[1,8192]{1,0:T(1,128)} %bitcast.6, bf16[2,8,2,128,128]{4,3,2,1,0:T(8,128)(2,1)} %kv.1, bf16[512,8192]{1,0:T(8,128)(2,1)} %w_own.1, bf16[8192,512]{1,0:T(8,128)(2,1)} %w_query.1), custom_call_target="tpu_custom_call" | custom-call | tf_op jit(solution)/shard_map/front/pallas_call | solution.py:288
  73.2 0.0 copy-start.1
  73.2 0.0 copy-done.3
  73.2 0.0 copy-done.5
  73.2 0.0 copy-done.6
  73.2 0.0 copy-done.7
  73.2 0.0 copy-done.8
  73.2 0.0 copy-start.2
  73.3 1.7 copy-done.2
  75.0 0.0 copy-start.4
  75.0 1.2 copy-done.4
  76.2 11.2 %mid.1.heads = bf16[384,512]{1,0:T(8,128)(2,1)S(1)} custom-call(s32[4,8]{1,0:T(4,128)S(1)} %copy-done.6, s32[4]{0:T(128)S(1)} %copy-done.7, s32[1]{0:T(128)} %bitcast.head, f32[384,512]{1,0:T(8,128)S(1)} %copy-done.4, s32[384,1]{1,0:T(8,128)S(1)} %reshape.16.depth_down, s32[4,1,96]{2,1,0:T(1,128)S(1)} %bitcast.5, f32[1,128]{1,0:T(1,128)S(1)} %copy-done.8, ...), custom_call_target="tpu_custom_call" | custom-call | tf_op jit(solution)/shard_map/mid/pallas_call | solution.py:623
  87.4 0.0 copy-done.1
  87.4 0.0 copy-start
  87.4 3.4 %copy-done = bf16[512,8192]{1,0:T(8,128)(2,1)S(1)} copy-done((bf16[512,8192]{1,0:T(8,128)(2,1)S(1)}, bf16[512,8192]{1,0:T(8,128)(2,1)}, u32[]{:S(2)}) %copy-start) | copy-done | bytes 8388632
  90.8 83.5 %back.1 = bf16[384,8192]{1,0:T(8,128)(2,1)S(1)} custom-call(bf16[384,512]{1,0:T(8,128)(2,1)S(1)} %mid.1.heads, bf16[512,8192]{1,0:T(8,128)(2,1)S(1)} %copy-done, bf16[512,4096]{1,0:T(8,128)(2,1)S(1)} %copy-done.1), custom_call_target="tpu_custom_call" | custom-call | tf_op jit(solution)/shard_map/back/pallas_call | solution.py:487
  174.3 2.7 %copy.13 = bf16[384,8192]{1,0:T(8,128)(2,1)} copy(bf16[384,8192]{1,0:T(8,128)(2,1)S(1)} %back.1) | data formatting | bytes 12582912
Async XLA Ops:
  0.9 72.3 %copy-start.3 = (bf16[384,2,1024]{2,1,0:T(2,128)(2,1)S(1)}, bf16[384,2,1024]{2,1,0:T(2,128)(2,1)}, u32[]{:S(2)}) copy-start(bf16[384,2,1024]{2,1,0:T(2,128)(2,1)} %draft_kv.1) | copy-start | bytes 4718596
  0.9 72.3 %copy-start.5 = (s32[4,96]{1,0:T(4,128)S(1)}, s32[4,96]{1,0:T(4,128)}, u32[]{:S(2)}) copy-start(s32[4,96]{1,0:T(4,128)} %param.18) | copy-start | bytes 4612
  0.9 72.3 %copy-start.6 = (s32[4,8]{1,0:T(4,128)S(1)}, s32[4,8]{1,0:T(4,128)}, u32[]{:S(2)}) copy-start(s32[4,8]{1,0:T(4,128)} %table.1) | copy-start | bytes 388
  0.9 72.3 %copy-start.7 = (s32[4]{0:T(128)S(1)}, s32[4]{0:T(128)}, u32[]{:S(2)}) copy-start(s32[4]{0:T(128)} %lengths.1) | copy-start | bytes 52
  0.9 72.3 %copy-start.8 = (f32[1,128]{1,0:T(1,128)S(1)}, f32[1,128]{1,0:T(1,128)}, u32[]{:S(2)}) copy-start(f32[1,128]{1,0:T(1,128)} %constant.29.frequency) | copy-start | bytes 1540
  73.2 14.2 %copy-start.1 = (bf16[512,4096]{1,0:T(8,128)(2,1)S(1)}, bf16[512,4096]{1,0:T(8,128)(2,1)}, u32[]{:S(2)}) copy-start(bf16[512,4096]{1,0:T(8,128)(2,1)} %get-tuple-element.10.w_mate) | copy-start | bytes 12582916
  73.2 1.7 copy-start.2
  75.0 1.2 copy-start.4
  87.4 3.4 %copy-start = (bf16[512,8192]{1,0:T(8,128)(2,1)S(1)}, bf16[512,8192]{1,0:T(8,128)(2,1)}, u32[]{:S(2)}) copy-start(bf16[512,8192]{1,0:T(8,128)(2,1)} %w_own.1) | copy-start | bytes 25165828

commit v6 on v5

--- a/solution.py
+++ b/solution.py
@@ -8,8 +8,8 @@
 from jax.experimental.pallas import tpu as pltpu
 from jax.sharding import PartitionSpec as P
 
-VMEM_LIMIT = 24 * 1024 * 1024
-FRONT_VMEM_LIMIT = 56 * 1024 * 1024
+VMEM_LIMIT = 40 * 1024 * 1024
+WIDE_VMEM_LIMIT = 56 * 1024 * 1024
 PIECES = 2
 
 
@@ -93,9 +93,11 @@
         src = rows(own, h) if s == 0 else here
         if s > 0:
             remote(here, here, zs.at[s - 1, h], zr.at[s - 1, h], at.previous).wait_recv()
-        if s < nz - 1:
+        if s < nz - 2:
             send(src, here, zs.at[s, h], zr.at[s, h], at.next)
-        if ny == 2:
+        if s == 0:
+            send(src, here, zs.at[nz - 2, h], zr.at[nz - 2, h], at.previous)
+        if ny == 2 and s < nz - 1:
             send(src, here, ys.at[s, h], yr.at[s, h], at.across)
         send(src, here, ms.at[s, h], mr.at[s, h], at.mate)
 
@@ -103,6 +105,8 @@
         if ny == 2:
             there = block(at.p, at.down(at.z, s), 1 - at.y, h)
             remote(there, there, ys.at[s, h], yr.at[s, h], at.across).wait_recv()
+            if s == 0:
+                send(there, there, ys.at[nz - 1, h], yr.at[nz - 1, h], at.previous)
             send(there, there, ms.at[nz + s, h], mr.at[nz + s, h], at.mate)
 
     def step(s, pieces=range(PIECES)):
@@ -311,7 +315,7 @@
         + [dma((2 * nz,)), dma((2 * nz,)), dma((2 * nz,)), dma((2 * nz,)), dma, dma, dma]
         + [dma((ranks,)), dma((ranks - 1,)), dma((ranks - 1,))],
         compiler_params=pltpu.CompilerParams(
-            collective_id=0, has_side_effects=True, vmem_limit_bytes=FRONT_VMEM_LIMIT
+            collective_id=0, has_side_effects=True, vmem_limit_bytes=WIDE_VMEM_LIMIT
         ),
         name="front",
     )(hidden, gain, kv_pool, w_out, w_query)
@@ -642,7 +646,7 @@
             ],
         ),
         compiler_params=pltpu.CompilerParams(
-            dimension_semantics=("arbitrary",), vmem_limit_bytes=VMEM_LIMIT
+            dimension_semantics=("arbitrary",), vmem_limit_bytes=WIDE_VMEM_LIMIT
         ),
         name="mid",
     )(

time: 177 us -> 180 us (1.017)
  Pallas kernels: 167 us -> 174 us
  local copies, waits for them, and re-layouts: 9.93 us -> 5.26 us
    pallas_call x1, Pallas kernels: 72.3 us -> 79.7 us  [front(): pl.pallas_call(functools.partial(front_kernel, ny, nt, group_size), out_s...]
    unnamed x19 -> x5, local copies, waits for them, and re-layouts: 9.08 us -> 3.7 us
where the time goes in v6:
time: 180 us; the launch traced here: 179 us
  Pallas kernels  174 us (97%)
  local copies, waits for them, and re-layouts  5.26 us (3%)
    pallas_call x1, Pallas kernels, back(): pl.pallas_call(functools.partial(back_kernel, ny, nt), out_shape=jax.Shap...  83.4 us
    pallas_call x1, Pallas kernels, front(): pl.pallas_call(functools.partial(front_kernel, ny, nt, group_size), out_s...  79.7 us
    pallas_call x1, Pallas kernels, attention(): pl.pallas_call(attention_kernel, out_shape=jax.ShapeDtypeStruct((rows, co...  11 us
    unnamed x5, local copies, waits for them, and re-layouts  3.7 us

profile of v6, /device:TPU:0, one launch (start us, length us, event | category | flops | bytes accessed | tf_op | source)
XLA Modules:
  0.0 179.4 jit_solution(8008870982841172396)
XLA Ops:
  0.0 1.6 reshape.16.depth_down
  1.6 79.7 %front.1 = (f32[384,512]{1,0:T(8,128)}, bf16[16,2,2,128,128]{4,3,2,1,0:T(8,128)(2,1)}, bf16[512,4096]{1,0:T(8,128)(2,1)}) custom-call(bf16[384,512]{1,0:T(8,128)(2,1)} %hidden.1, f32[1,8192]{1,0:T(1,128)} %bitcast.5, bf16[2,8,2,128,128]{4,3,2,1,0:T(8,128)(2,1)} %kv.1, bf16[512,8192]{1,0:T(8,128)(2,1)} %w_own.1, bf16[8192,512]{1,0:T(8,128)(2,1)} %w_query.1), custom_call_target="tpu_custom_call" | custom-call | tf_op jit(solution)/shard_map/front/pallas_call | solution.py:292
  81.2 0.0 copy-start
  81.2 11.0 %mid.1.heads = bf16[384,512]{1,0:T(8,128)(2,1)} custom-call(s32[4,8]{1,0:T(4,128)} %table.1, s32[4]{0:T(128)} %lengths.1, s32[1]{0:T(128)} %bitcast.head, f32[384,512]{1,0:T(8,128)} %get-tuple-element.8.raw, s32[384,1]{1,0:T(8,128)} %reshape.16.depth_down, s32[4,1,96]{2,1,0:T(1,128)} %bitcast.6, f32[1,128]{1,0:T(1,128)} %constant.29.frequency, ...), custom_call_target="tpu_custom_call" | custom-call | tf_op jit(solution)/shard_map/mid/pallas_call | solution.py:627
  92.3 0.0 copy-done
  92.3 0.0 copy-start.1
  92.3 1.0 copy-done.1
  93.3 83.4 %back.1 = bf16[384,8192]{1,0:T(8,128)(2,1)S(1)} custom-call(bf16[384,512]{1,0:T(8,128)(2,1)S(1)} %copy-done.1, bf16[512,8192]{1,0:T(8,128)(2,1)} %w_own.1, bf16[512,4096]{1,0:T(8,128)(2,1)S(1)} %copy-done), custom_call_target="tpu_custom_call" | custom-call | tf_op jit(solution)/shard_map/back/pallas_call | solution.py:491
  176.7 2.7 %copy.13 = bf16[384,8192]{1,0:T(8,128)(2,1)} copy(bf16[384,8192]{1,0:T(8,128)(2,1)S(1)} %back.1) | data formatting | bytes 12582912
Async XLA Ops:
  81.2 11.0 %copy-start = (bf16[512,4096]{1,0:T(8,128)(2,1)S(1)}, bf16[512,4096]{1,0:T(8,128)(2,1)}, u32[]{:S(2)}) copy-start(bf16[512,4096]{1,0:T(8,128)(2,1)} %get-tuple-element.10.w_mate) | copy-start | bytes 12582916
  92.3 1.0 copy-start.1

commit v7 on v6

--- a/solution.py
+++ b/solution.py
@@ -93,11 +93,9 @@
         src = rows(own, h) if s == 0 else here
         if s > 0:
             remote(here, here, zs.at[s - 1, h], zr.at[s - 1, h], at.previous).wait_recv()
-        if s < nz - 2:
+        if s < nz - 1:
             send(src, here, zs.at[s, h], zr.at[s, h], at.next)
-        if s == 0:
-            send(src, here, zs.at[nz - 2, h], zr.at[nz - 2, h], at.previous)
-        if ny == 2 and s < nz - 1:
+        if ny == 2:
             send(src, here, ys.at[s, h], yr.at[s, h], at.across)
         send(src, here, ms.at[s, h], mr.at[s, h], at.mate)
 
@@ -105,8 +103,6 @@
         if ny == 2:
             there = block(at.p, at.down(at.z, s), 1 - at.y, h)
             remote(there, there, ys.at[s, h], yr.at[s, h], at.across).wait_recv()
-            if s == 0:
-                send(there, there, ys.at[nz - 1, h], yr.at[nz - 1, h], at.previous)
             send(there, there, ms.at[nz + s, h], mr.at[nz + s, h], at.mate)
 
     def step(s, pieces=range(PIECES)):

time: 180 us -> 172 us (0.956)
  Pallas kernels: 174 us -> 166 us
    pallas_call x1, Pallas kernels: 79.7 us -> 72.1 us  [front(): pl.pallas_call(functools.partial(front_kernel, ny, nt, group_size), out_s...]
where the time goes in v7:
time: 172 us; the launch traced here: 171 us
  Pallas kernels  166 us (97%)
  local copies, waits for them, and re-layouts  5.26 us (3%)
    pallas_call x1, Pallas kernels, back(): pl.pallas_call(functools.partial(back_kernel, ny, nt), out_shape=jax.Shap...  82.9 us
    pallas_call x1, Pallas kernels, front(): pl.pallas_call(functools.partial(front_kernel, ny, nt, group_size), out_s...  72.1 us
    pallas_call x1, Pallas kernels, attention(): pl.pallas_call(attention_kernel, out_shape=jax.ShapeDtypeStruct((rows, co...  11 us
    unnamed x5, local copies, waits for them, and re-layouts  3.7 us

profile of v7, /device:TPU:0, one launch (start us, length us, event | category | flops | bytes accessed | tf_op | source)
XLA Modules:
  0.0 171.3 jit_solution(2318358778528274207)
XLA Ops:
  0.0 1.6 reshape.16.depth_down
  1.6 72.1 %front.1 = (f32[384,512]{1,0:T(8,128)}, bf16[16,2,2,128,128]{4,3,2,1,0:T(8,128)(2,1)}, bf16[512,4096]{1,0:T(8,128)(2,1)}) custom-call(bf16[384,512]{1,0:T(8,128)(2,1)} %hidden.1, f32[1,8192]{1,0:T(1,128)} %bitcast.5, bf16[2,8,2,128,128]{4,3,2,1,0:T(8,128)(2,1)} %kv.1, bf16[512,8192]{1,0:T(8,128)(2,1)} %w_own.1, bf16[8192,512]{1,0:T(8,128)(2,1)} %w_query.1), custom_call_target="tpu_custom_call" | custom-call | tf_op jit(solution)/shard_map/front/pallas_call | solution.py:288
  73.7 0.0 copy-start
  73.7 11.0 %mid.1.heads = bf16[384,512]{1,0:T(8,128)(2,1)} custom-call(s32[4,8]{1,0:T(4,128)} %table.1, s32[4]{0:T(128)} %lengths.1, s32[1]{0:T(128)} %bitcast.head, f32[384,512]{1,0:T(8,128)} %get-tuple-element.8.raw, s32[384,1]{1,0:T(8,128)} %reshape.16.depth_down, s32[4,1,96]{2,1,0:T(1,128)} %bitcast.6, f32[1,128]{1,0:T(1,128)} %constant.29.frequency, ...), custom_call_target="tpu_custom_call" | custom-call | tf_op jit(solution)/shard_map/mid/pallas_call | solution.py:623
  84.7 0.0 copy-done
  84.7 0.0 copy-start.1
  84.7 1.0 copy-done.1
  85.7 82.9 %back.1 = bf16[384,8192]{1,0:T(8,128)(2,1)S(1)} custom-call(bf16[384,512]{1,0:T(8,128)(2,1)S(1)} %copy-done.1, bf16[512,8192]{1,0:T(8,128)(2,1)} %w_own.1, bf16[512,4096]{1,0:T(8,128)(2,1)S(1)} %copy-done), custom_call_target="tpu_custom_call" | custom-call | tf_op jit(solution)/shard_map/back/pallas_call | solution.py:487
  168.6 2.7 %copy.13 = bf16[384,8192]{1,0:T(8,128)(2,1)} copy(bf16[384,8192]{1,0:T(8,128)(2,1)S(1)} %back.1) | data formatting | bytes 12582912
Async XLA Ops:
  73.7 11.0 %copy-start = (bf16[512,4096]{1,0:T(8,128)(2,1)S(1)}, bf16[512,4096]{1,0:T(8,128)(2,1)}, u32[]{:S(2)}) copy-start(bf16[512,4096]{1,0:T(8,128)(2,1)} %get-tuple-element.10.w_mate) | copy-start | bytes 12582916
  84.7 1.0 copy-start.1
